TPU v7x, 128 devices: a whole 4x4x4 slice. The times are simulated.
128 devices in a mesh: dev: 128 (over x, z, y, core).
Axes of the slice: x: 4, y: 4, z: 4, core: 2. Of those that a mesh axis runs over, the one named last changes fastest.
Arguments:
- embeddings: bfloat16 [256, 128, 1280], P('dev')
- lengths: int32 [256], replicated, may hold values from 16 to 128, as said below
- pairs: int32 [128, 2], replicated, may hold values from 0 to 255, as said below
- labels: int32 [128], P('dev'), may hold values 0 or 1
- w_query: bfloat16 [1280, 1280], replicated, may hold values from -0.15625 to 0.15625
- w_key: bfloat16 [1280, 1280], replicated, may hold values from -0.15625 to 0.15625
- w_value: bfloat16 [1280, 1280], replicated, may hold values from -0.15625 to 0.15625
- w_out: bfloat16 [1280, 1280], replicated, may hold values from -0.15625 to 0.15625
- w_class: float32 [1280], replicated, may hold values from -4 to 4
Outputs:
- d_embeddings: float32 [256, 128, 1280], P('dev')
- d_weights: float32 [1280, 4, 1280], P('dev')
Inputs may be any that keep to these rules, and one draw needn't show every extreme that they name: `pairs`: the two ids of a pair differ. `lengths`: some chain has exactly 128 residues.
All inputs are finite; a program needn't handle non-finite values. No bound on the sum of `labels` on one device may be relied on, other than what follows from the above.
Results may differ from a plain program's by a relative error of at most 0.013.
Values may be sent and summed in bfloat16 or wider, within the bound.
No kernel may reach another device: no remote copies, remote signals or barrier semaphores. Data moves between devices by JAX's collectives and lax.ppermute only.
A program may use at most 192 MiB of HBM per device.

v0:
```python
import jax
import jax.numpy as jnp
from jax import lax
from jax.sharding import PartitionSpec as P

HEADS = 16


def attend(query, keys, values, key_lens):
    npair, sides, length, width = query.shape
    head_dim = width // HEADS
    qh = query.reshape(npair, sides, length, HEADS, head_dim).astype(jnp.float32)
    kh = keys.reshape(npair, sides, length, HEADS, head_dim).astype(jnp.float32)
    vh = values.reshape(npair, sides, length, HEADS, head_dim).astype(jnp.float32)
    scores = jnp.einsum("psqhd,pskhd->pshqk", qh, kh) * head_dim ** (-0.5)
    slots = jnp.arange(length, dtype=jnp.int32)
    key_valid = slots[None, None, None, None, :] < key_lens[:, :, None, None, None]
    scores = jnp.where(key_valid, scores, -1000000000.0)
    scores = scores - jnp.max(scores, axis=-1, keepdims=True)
    expo = jnp.exp(scores)
    probs = (expo / jnp.sum(expo, axis=-1, keepdims=True)).astype(jnp.bfloat16)
    context = jnp.einsum("pshqk,pskhd->psqhd", probs.astype(jnp.float32), vh)
    return context.reshape(npair, sides, length, width).astype(jnp.bfloat16)


def forward_backward(chains, chain_lens, pair_labels, w_query, w_key, w_value, w_out, w_class):
    npair, sides, length, width = chains.shape
    flat_x = chains.reshape(-1, width)
    query = (
        jnp.dot(flat_x, w_query, preferred_element_type=jnp.float32)
        .astype(jnp.bfloat16)
        .reshape(chains.shape)
    )
    keys = (
        jnp.dot(flat_x, w_key, preferred_element_type=jnp.float32)
        .astype(jnp.bfloat16)
        .reshape(chains.shape)
    )
    values = (
        jnp.dot(flat_x, w_value, preferred_element_type=jnp.float32)
        .astype(jnp.bfloat16)
        .reshape(chains.shape)
    )
    other_lens = chain_lens[:, ::-1]

    def attention(q_in, k_in, v_in):
        return attend(q_in, k_in, v_in, other_lens)

    context, attention_back = jax.vjp(attention, query, keys[:, ::-1], values[:, ::-1])
    flat_ctx = context.reshape(-1, width)
    outputs = jnp.dot(flat_ctx, w_out, preferred_element_type=jnp.float32).reshape(chains.shape)
    slots = jnp.arange(length, dtype=jnp.int32)
    valid = (slots[None, None, :] < chain_lens[:, :, None]).astype(jnp.float32)
    lens_float = chain_lens.astype(jnp.float32)
    mixed = chains.astype(jnp.float32) + outputs
    pooled = jnp.sum(mixed * valid[..., None], axis=2) / lens_float[..., None]
    logits = jnp.sum(w_class[None, :] * pooled[:, 0] * pooled[:, 1], axis=-1)
    slope = jax.nn.sigmoid(logits) - pair_labels.astype(jnp.float32)
    d_pooled = slope[:, None, None] * w_class[None, None, :] * pooled[:, ::-1]
    d_mixed = valid[..., None] * (d_pooled / lens_float[..., None])[:, :, None, :]
    d_out = d_mixed.astype(jnp.bfloat16).reshape(-1, width)
    d_ctx = lax.dot_general(
        d_out, w_out, (((1,), (1,)), ((), ())), preferred_element_type=jnp.float32
    )
    d_ctx = d_ctx.astype(jnp.bfloat16).reshape(chains.shape)
    d_query, d_keys_other, d_values_other = attention_back(d_ctx)
    d_keys = d_keys_other[:, ::-1]
    d_values = d_values_other[:, ::-1]
    grads_three = jnp.concatenate(
        [d_query.reshape(-1, width), d_keys.reshape(-1, width), d_values.reshape(-1, width)], axis=1
    )
    stacked = jnp.concatenate([w_query, w_key, w_value], axis=1)
    back_in = lax.dot_general(
        grads_three, stacked, (((1,), (1,)), ((), ())), preferred_element_type=jnp.float32
    )
    d_input = d_mixed + back_in.reshape(chains.shape)
    return (d_input, flat_x, grads_three, flat_ctx, d_out)


def weight_grads(flat_x, grads_three, flat_ctx, d_out):
    upper = lax.dot_general(
        flat_x, grads_three, (((0,), (0,)), ((), ())), preferred_element_type=jnp.float32
    )
    lower = lax.dot_general(
        flat_ctx, d_out, (((0,), (0,)), ((), ())), preferred_element_type=jnp.float32
    )
    joined = jnp.concatenate([upper, lower], axis=1)
    return joined.reshape(flat_x.shape[1], 4, d_out.shape[1])


def shards(embeddings, lengths, pairs, labels, w_query, w_key, w_value, w_out, w_class):
    pair_dev = labels.shape[0]
    length = embeddings.shape[1]
    width = embeddings.shape[2]
    chain_total = lengths.shape[0]
    spread = lax.all_to_all(embeddings, "dev", split_axis=1, concat_axis=0, tiled=True)
    slot_ids = pairs.reshape(-1)
    picked = jnp.take(spread, slot_ids, axis=0)
    gathered = lax.all_to_all(picked, "dev", split_axis=0, concat_axis=1, tiled=True)
    chains = gathered.reshape(pair_dev, 2, length, width)
    first_pair = lax.axis_index("dev") * pair_dev
    my_pairs = lax.dynamic_slice_in_dim(pairs, first_pair, pair_dev, 0)
    chain_lens = jnp.take(lengths, my_pairs, axis=0)
    d_input, flat_x, grads_three, flat_ctx, d_out = forward_backward(
        chains, chain_lens, labels, w_query, w_key, w_value, w_out, w_class
    )
    d_weights = lax.psum_scatter(
        weight_grads(flat_x, grads_three, flat_ctx, d_out), "dev", scatter_dimension=0, tiled=True
    )
    slot_grads = d_input.reshape(2 * pair_dev, length, width)
    by_rows = lax.all_to_all(slot_grads, "dev", split_axis=1, concat_axis=0, tiled=True)
    row_block = by_rows.shape[1]
    chain_index = jnp.arange(chain_total, dtype=jnp.int32)
    selector = (chain_index[:, None] == slot_ids[None, :]).astype(jnp.float32)
    summed = jnp.dot(
        selector,
        by_rows.reshape(slot_ids.shape[0], row_block * width),
        precision=lax.Precision.HIGHEST,
        preferred_element_type=jnp.float32,
    )
    summed = summed.reshape(chain_total, row_block, width)
    d_embeddings = lax.all_to_all(summed, "dev", split_axis=0, concat_axis=1, tiled=True)
    return (d_embeddings, d_weights)


def solution(mesh):
    placed = (P("dev", None, None), P(), P(), P("dev"), P(), P(), P(), P(), P())
    return jax.shard_map(
        shards,
        mesh=mesh,
        in_specs=placed,
        out_specs=(P("dev", None, None), P("dev", None, None)),
        check_vma=False,
    )
```

profile of v0, /device:TPU:1, one launch (start us, length us, event | category | flops | bytes accessed | tf_op | source)
XLA Modules:
  0.0 453.9 jit_solution(7123961429486814008)
XLA Ops:
  7.2 2.7 copy.57
  10.0 11.9 %all-to-all-start = ((bf16[2,128,1280]{2,0,1:T(2,128)(2,1)}), bf16[2,128,1280]{2,0,1:T(2,128)(2,1)}, u32[]{:S(2)}, u32[]{:S(2)}) async-start(bf16[2,128,1280]{2,0,1:T(2,128)(2,1)} %copy.57), calls=%async_computation | async-start | bytes 1310720 | tf_op jit(solution)/shard_map/all_to_all | solution.py:96
  23.0 13.5 %all-to-all-done = bf16[2,128,1280]{2,0,1:T(2,128)(2,1)} async-done(((bf16[2,128,1280]{2,0,1:T(2,128)(2,1)}), bf16[2,128,1280]{2,0,1:T(2,128)(2,1)}, u32[]{:S(2)}, u32[]{:S(2)}) %all-to-all-start) | async-done | bytes 655392 | tf_op jit(solution)/shard_map/all_to_all | solution.py:96
  39.2 3.8 gather_fusion.1
  45.5 2.9 reduce.19
  51.0 5.5 %all-to-all-start.1 = ((bf16[128,2,1280]{2,1,0:T(2,128)(2,1)}), bf16[128,2,1280]{2,1,0:T(2,128)(2,1)}, u32[]{:S(2)}, u32[]{:S(2)}) async-start(bf16[128,2,1280]{2,1,0:T(2,128)(2,1)} %reshape.436), calls=%async_computation.1 | async-start | bytes 1310720 | tf_op jit(solution)/shard_map/all_to_all | solution.py:99
  57.8 13.5 %all-to-all-done.1 = bf16[128,2,1280]{2,1,0:T(2,128)(2,1)} async-done(((bf16[128,2,1280]{2,1,0:T(2,128)(2,1)}), bf16[128,2,1280]{2,1,0:T(2,128)(2,1)}, u32[]{:S(2)}, u32[]{:S(2)}) %all-to-all-start.1) | async-done | bytes 655392 | tf_op jit(solution)/shard_map/all_to_all | solution.py:99
  71.3 5.1 %reshape.437 = bf16[256,1,1280]{2,1,0:T(2,128)(2,1)} reshape(bf16[128,2,1280]{2,1,0:T(2,128)(2,1)} %all-to-all-done.1) | data formatting | bytes 1310720
  76.4 5.8 %reduce.14 = bf16[256,1280]{1,0:T(8,128)(2,1)} reduce(bf16[256,1,1280]{2,1,0:T(2,128)(2,1)} %reshape.437, bf16[]{:T(256)} %constant.57), dimensions={1}, to_apply=%all_to_all.52.reduce_sub_computation | reduce | bytes 1310722 | tf_op jit(solution)/shard_map/all_to_all | solution.py:99
  86.8 3.8 convolution_convert_fusion.2
  90.6 3.3 reshape.432
  93.9 3.1 copy.64
  97.0 4.0 convolution_convert_fusion.1
  125.6 2.8 reshape.397
  128.5 2.9 convolution_convert_fusion.5
  137.7 3.8 convolution_bitcast_fusion
  145.1 2.8 fusion.32
  147.9 11.8 %pad_maximum_fusion = f32[1280,5120]{1,0:T(8,128)} fusion(f32[1280,1280]{1,0:T(8,128)} %convolution_bitcast_fusion, f32[1280,3840]{1,0:T(8,128)S(1)} %fusion.32), kind=kLoop, calls=%fused_computation.2 | loop fusion | flops 6553600 | bytes 52428800 | tf_op jit(solution)/shard_map/concatenate | solution.py:87
  159.7 31.9 %reshape.407 = f32[1280,4,1280]{2,1,0:T(4,128)} reshape(f32[1280,5120]{1,0:T(8,128)} %pad_maximum_fusion) | data formatting | bytes 52428800 | tf_op jit(solution)/shard_map/reshape | solution.py:88
  191.6 6.2 %fusion = f32[256,1280]{1,0:T(8,128)S(1)} fusion(bf16[1280,1280]{1,0:T(8,128)(2,1)} %param.15, bf16[1280,1280]{1,0:T(8,128)(2,1)} %param.14, bf16[1280,1280]{1,0:T(8,128)(2,1)} %param.13, bf16[256,1280]{0,1:T(8,128)(2,1)S(1)} %copy.78, bf16[256,1280]{0,1:T(8,128)(2,1)S(1)} %copy.77, bf16[256,1280]{0,1:T(8,128)(2,1)S(1)} %bitcast.130), kind=kOutput, calls=%fused_computation.3 | convolution fusion | flops 2551971840 | bytes 13107200 | tf_op jit(solution)/shard_map/dot_general | solution.py:73
  199.0 30.9 %all_to_all.66 = f32[2,128,1280]{2,0,1:T(2,128)} all-to-all(f32[2,128,1280]{2,0,1:T(2,128)S(1)} %copy.79), channel_id=1, replica_groups=mesh['dev'=128] {'dev'}, dimensions={1} | all-to-all | bytes 2621440 | tf_op jit(solution)/shard_map/all_to_all | solution.py:111
  235.4 5.9 %all-to-all-start.3 = ((f32[256,1,1280]{2,1,0:T(1,128)}), f32[256,1,1280]{2,1,0:T(1,128)}, u32[]{:S(2)}, u32[]{:S(2)}) async-start(f32[256,1,1280]{2,1,0:T(1,128)} %copy.80), calls=%async_computation.3 | async-start | bytes 2621440 | tf_op jit(solution)/shard_map/all_to_all | solution.py:122
  241.3 25.9 %all-to-all-done.3 = f32[256,1,1280]{2,1,0:T(1,128)} async-done(((f32[256,1,1280]{2,1,0:T(1,128)}), f32[256,1,1280]{2,1,0:T(1,128)}, u32[]{:S(2)}, u32[]{:S(2)}) %all-to-all-start.3) | async-done | bytes 1310752 | tf_op jit(solution)/shard_map/all_to_all | solution.py:122
  269.8 175.4 %all-reduce.3.cloned.1.call-done = f32[1280,4,1280]{2,1,0:T(4,128)} async-done(((f32[1280,4,1280]{2,1,0:T(4,128)}), f32[1280,4,1280]{2,1,0:T(4,128)}) %all-reduce.3.cloned.1.call-update) | async-done | bytes 26214416
  (104 shorter events, 58.6 us)
Async XLA Ops:
  7.2 111.2 %copy-start = (bf16[1280,1280]{1,0:T(8,128)(2,1)S(1)}, bf16[1280,1280]{1,0:T(8,128)(2,1)}, u32[]{:S(2)}) copy-start(bf16[1280,1280]{1,0:T(8,128)(2,1)} %param.16) | copy-start | bytes 9830404
  7.2 14.7 %copy-start.19 = (s32[128,2]{0,1:T(2,128)S(1)}, s32[128,2]{0,1:T(2,128)}, u32[]{:S(2)}) copy-start(s32[128,2]{0,1:T(2,128)} %param.11) | copy-start | bytes 3076
  7.2 15.1 %copy-start.2 = (s32[256]{0:T(256)S(1)}, s32[256]{0:T(256)}, u32[]{:S(2)}) copy-start(s32[256]{0:T(256)} %param.10) | copy-start | bytes 3076
  10.0 26.5 %all-to-all-start = ((bf16[2,128,1280]{2,0,1:T(2,128)(2,1)}), bf16[2,128,1280]{2,0,1:T(2,128)(2,1)}, u32[]{:S(2)}, u32[]{:S(2)}) async-start(bf16[2,128,1280]{2,0,1:T(2,128)(2,1)} %copy.57), calls=%async_computation | async-start | bytes 1310720 | tf_op jit(solution)/shard_map/all_to_all | solution.py:96
  51.0 20.3 %all-to-all-start.1 = ((bf16[128,2,1280]{2,1,0:T(2,128)(2,1)}), bf16[128,2,1280]{2,1,0:T(2,128)(2,1)}, u32[]{:S(2)}, u32[]{:S(2)}) async-start(bf16[128,2,1280]{2,1,0:T(2,128)(2,1)} %reshape.436), calls=%async_computation.1 | async-start | bytes 1310720 | tf_op jit(solution)/shard_map/all_to_all | solution.py:99
  56.6 388.6 %all-reduce.3.cloned.1.call-start = ((), (), s32[]{:S(2)}) async-start(), calls=%async_computation.4 | async-start | bytes 52428800
  107.2 1.8 copy-start.3
  107.2 3.1 copy-start.20
  107.6 2.8 copy-start.11
  116.4 2.0 copy-start.14
  118.3 1.1 copy-start.8
  118.4 1.5 copy-start.18
  123.3 5.1 %copy-start.5 = (bf16[2,16,128,128]{2,3,1,0:T(8,128)(2,1)S(1)}, bf16[2,16,128,128]{2,3,1,0:T(8,128)(2,1)}, u32[]{:S(2)}) copy-start(bf16[2,16,128,128]{2,3,1,0:T(8,128)(2,1)} %divide_convert_fusion) | copy-start | bytes 3145732
  125.6 5.7 %copy-start.4 = (f32[2,16,128,128]{2,3,1,0:T(8,128)S(1)}, f32[2,16,128,128]{2,3,1,0:T(8,128)}, u32[]{:S(2)}) copy-start(f32[2,16,128,128]{2,3,1,0:T(8,128)} %copy-done.3) | copy-start | bytes 6291460
  128.5 2.9 copy-start.6
  128.5 2.9 copy-start.7
  132.2 1.3 copy-start.15
  133.5 2.2 copy-start.16
  135.7 2.0 copy-start.9
  137.7 3.8 copy-start.13
  141.5 1.1 copy-start.17
  142.9 2.1 copy-start.12
  235.4 31.9 %all-to-all-start.3 = ((f32[256,1,1280]{2,1,0:T(1,128)}), f32[256,1,1280]{2,1,0:T(1,128)}, u32[]{:S(2)}, u32[]{:S(2)}) async-start(f32[256,1,1280]{2,1,0:T(1,128)} %copy.80), calls=%async_computation.3 | async-start | bytes 2621440 | tf_op jit(solution)/shard_map/all_to_all | solution.py:122
  241.3 205.5 %copy-start.1 = (bf16[1280,1280]{1,0:T(8,128)(2,1)S(1)}, bf16[1280,1280]{1,0:T(8,128)(2,1)}, u32[]{:S(2)}) copy-start(bf16[1280,1280]{1,0:T(8,128)(2,1)} %param.16) | copy-start | bytes 9830404
  (1 other events, 0.9 us)
Sparse Core Ops, SparseCore 0:
  191.7 253.3 all-reduce.2
where the time goes:
time: 461 us; the launch traced here: 454 us
  waiting for transfers between devices  228 us (49%)
  local copies, waits for them, and re-layouts  89.9 us (20%)
  matrix products  38.1 us (8%)
  blocking collectives  30.9 us (7%)
  other arithmetic  26.9 us (6%)
  starting transfers between devices  23.7 us (5%)
  between operations  16.1 us (3%)
    unnamed x2, waiting for transfers between devices  175 us
    reshape x1, local copies, waits for them, and re-layouts, weight_grads(): return joined.reshape(flat_x.shape[1], 4, d_out.shape[1])  31.9 us
    all_to_all x1, blocking collectives, shards(): lax.all_to_all(slot_grads, 'dev', split_axis=1, concat_axis=0, tiled=True)  30.9 us
    all_to_all x1, waiting for transfers between devices, shards(): lax.all_to_all(summed, 'dev', split_axis=0, concat_axis=1, tiled=True)  25.9 us
    unnamed x48, local copies, waits for them, and re-layouts  15.2 us
    all_to_all x1, waiting for transfers between devices, shards(): lax.all_to_all(picked, 'dev', split_axis=0, concat_axis=1, tiled=True)  13.5 us
    all_to_all x1, waiting for transfers between devices, shards(): lax.all_to_all(embeddings, 'dev', split_axis=1, concat_axis=0, tiled=True)  13.5 us
    all_to_all x1, starting transfers between devices, shards(): lax.all_to_all(embeddings, 'dev', split_axis=1, concat_axis=0, tiled=True)  11.9 us
  transfers between devices with their start and end apart: 4, of which 4 were waited for; matrix products, arithmetic and copies ran while one was open for 4% of the time, Pallas kernels for 0%

commit v1 on v0

v1 whole, which is shorter than its diff:
```python
import functools

import jax
import jax.numpy as jnp
from jax import lax
from jax.experimental import pallas as pl
from jax.experimental.pallas import tpu as pltpu
from jax.sharding import PartitionSpec as P

HEADS = 16
HD = 80
L = 128
D = 1280
NDEV = 128
WINDOWS = (0, 256, 640, 896)
WIN = 384
BF = jnp.bfloat16
F32 = jnp.float32
NN = (((1,), (0,)), ((), ()))
NT = (((1,), (1,)), ((), ()))
TN = (((0,), (0,)), ((), ()))


def mm(a, b, dims=NN):
    return lax.dot_general(a, b, dims, preferred_element_type=F32)


def iota(shape, dim):
    return lax.broadcasted_iota(jnp.int32, shape, dim)


def split(a):
    hi = a.astype(BF)
    return hi, (a - hi.astype(F32)).astype(BF)


def pair_kernel(
    lengths, pairs, label, x, wc, wq_h, wk_h, wv_h, wo_h,
    mine, other, dx, z, dv,
    wq, wk, wv, wo, q, k, p, s, u, dq, dk, dqb, dkb, sems,
):
    dev = lax.axis_index("dev")
    core = dev % 2
    loads = []
    for n, (src, dst) in enumerate(((wq_h, wq), (wk_h, wk), (wv_h, wv), (wo_h, wo))):
        load = pltpu.make_async_copy(src, dst, sems.at[n])
        load.start()
        loads.append(load)
    lens = [lengths[pairs[2 * dev]], lengths[pairs[2 * dev + 1]]]
    rows = iota((L, L), 0)
    lanes = iota((L, L), 1)
    scale = HD ** (-0.5)

    loads[0].wait()
    for n in range(5):
        cols = slice(256 * n, 256 * n + 256)
        q[:, cols] = mm(x[...], wq[:, cols]).astype(BF)
    loads[1].wait()
    for n in range(5):
        cols = slice(256 * n, 256 * n + 256)
        k[:, cols] = mm(x[...], wk[:, cols]).astype(BF)

    spans = []
    for h in range(HEADS):
        low = HD * h
        first = low // 128 * 128
        last = (low + HD - 1) // 128 * 128 + 128
        spans.append((low, first, last))

    for h, (low, first, last) in enumerate(spans):
        lane = iota((L, last - first), 1) + first
        inside = jnp.where((lane >= low) & (lane < low + HD), 1.0, 0.0).astype(BF)
        for a in range(2):
            b = 1 - a
            qt = q[L * a : L * a + L, first:last] * inside
            scores = mm(qt, k[L * b : L * b + L, first:last], NT) * scale
            scores = jnp.where(lanes < lens[b], scores, -1000000000.0)
            expo = jnp.exp(scores - jnp.max(scores, axis=1, keepdims=True))
            prob = expo / jnp.sum(expo, axis=1, keepdims=True)
            prob = jnp.where(rows < lens[a], prob, 0.0)
            p[a * HEADS + h] = prob
            s[a * HEADS + h : a * HEADS + h + 1, :] = jnp.sum(
                prob.astype(BF).astype(F32), axis=0, keepdims=True
            )

    head_lane = iota((HEADS, D), 1)
    head_row = iota((HEADS, D), 0)
    headmask = (head_lane >= HD * head_row) & (head_lane < HD * head_row + HD)
    ys = []
    for a in range(2):
        b = 1 - a
        hi, lo = split(s[a * HEADS : a * HEADS + HEADS, :])
        ys.append(mm(hi, x[L * b : L * b + L, :]) + mm(lo, x[L * b : L * b + L, :]))
    y = jnp.concatenate(ys, axis=0)
    y_hi, y_lo = split(y)
    loads[2].wait()
    t = mm(y_hi, wv[...]) + mm(y_lo, wv[...])
    pooled_ctx = [
        jnp.sum(jnp.where(headmask, t[HEADS * a : HEADS * a + HEADS, :], 0.0), axis=0, keepdims=True)
        for a in range(2)
    ]
    row8 = iota((8, D), 0)
    ctx8 = jnp.where(row8 == 0, pooled_ctx[0], jnp.where(row8 == 1, pooled_ctx[1], 0.0))
    z[...] = jnp.concatenate([y, ctx8], axis=0).astype(BF)
    mask_row = iota((8, 2 * L), 0)
    mask_lane = iota((8, 2 * L), 1)
    mask8 = ((mask_row == 0) & (mask_lane < lens[0])) | (
        (mask_row == 1) & (mask_lane >= L) & (mask_lane < L + lens[1])
    )
    x_sum = mm(jnp.where(mask8, 1.0, 0.0).astype(BF), x[...])
    ctx_hi, ctx_lo = split(ctx8)
    loads[3].wait()
    total = x_sum + mm(ctx_hi, wo[...]) + mm(ctx_lo, wo[...])
    lens_f = [n.astype(F32) for n in lens]
    pooled = [total[0:1, :] / lens_f[0], total[1:2, :] / lens_f[1]]
    logit = jnp.sum(wc[...] * pooled[0] * pooled[1], axis=1, keepdims=True)
    slope = 1.0 / (1.0 + jnp.exp(-logit)) - label[0].astype(F32)
    dvec = [slope * wc[...] * pooled[1 - a] / lens_f[a] for a in range(2)]
    dvec8 = jnp.where(row8 == 0, dvec[0], jnp.where(row8 == 1, dvec[1], 0.0)).astype(BF)
    dv[:, 0:D] = dvec[0].astype(BF)
    dv[:, D : 2 * D] = dvec[1].astype(BF)
    g = mm(dvec8, wo[...], NT).astype(BF).astype(F32)
    gm = jnp.concatenate(
        [jnp.where(headmask, g[a : a + 1, :], 0.0) for a in range(2)], axis=0
    ).astype(BF)
    gv = mm(gm, wv[...], NT)
    gv_hi, gv_lo = split(gv)
    for a in range(2):
        b = 1 - a
        part = slice(HEADS * a, HEADS * a + HEADS)
        xb = x[L * b : L * b + L, :]
        u[part, :] = mm(gv_hi[part, :], xb, NT) + mm(gv_lo[part, :], xb, NT)

    for h, (low, first, last) in enumerate(spans):
        keep = lanes + first >= low
        for a in range(2):
            b = 1 - a
            row = a * HEADS + h
            prob = p[row]
            uh = u[row : row + 1, :]
            mean = jnp.sum(prob * uh, axis=1, keepdims=True)
            ds = (prob * (uh - mean) * scale).astype(BF)
            for out, side, val in (
                (dq, a, mm(ds, k[L * b : L * b + L, first:last])),
                (dk, b, mm(ds, q[L * a : L * a + L, first:last], TN)),
            ):
                here = slice(L * side, L * side + L)
                head = val[:, 0:128]
                if low > first:
                    head = jnp.where(keep, head, out[here, first : first + 128])
                out[here, first : first + 128] = head
                if last - first > 128:
                    out[here, first + 128 : last] = val[:, 128:]

    dqb[...] = dq[...].astype(BF)
    dkb[...] = dk[...].astype(BF)
    for w, start in enumerate(WINDOWS):
        cols = slice(start, start + WIN)
        even = core == 0
        mine[w] = jnp.where(even, dq[:, cols], dk[:, cols]).astype(BF)
        other[w] = jnp.where(even, dk[:, cols], dq[:, cols]).astype(BF)

    to = iota((2 * L, 2 * L), 0)
    frm = iota((2 * L, 2 * L), 1)
    weave = jnp.where(frm == (to & 1) * L + (to >> 1), 1.0, 0.0).astype(BF)
    s_b = s[...].astype(BF)
    tall = iota((L, 256), 0)
    for n in range(5):
        cols = slice(256 * n, 256 * n + 256)
        acc = mm(dqb[...], wq[cols, :], NT) + mm(dkb[...], wk[cols, :], NT)
        sides = []
        for c in range(2):
            a = 1 - c
            part = slice(HEADS * a, HEADS * a + HEADS)
            low_rank = mm(s_b[part, :], gv_hi[part, cols], TN)
            sides.append(low_rank + jnp.where(tall < lens[c], dvec[c][:, cols], 0.0))
        acc = acc + jnp.concatenate(sides, axis=0)
        dx[:, cols] = mm(weave, acc.astype(BF)).astype(BF)


def pair_step(lengths, pairs, label, x, wc, wq, wk, wv, wo):
    smem = pl.BlockSpec(memory_space=pltpu.SMEM)
    vmem = pl.BlockSpec(memory_space=pltpu.VMEM)
    hbm = pl.BlockSpec(memory_space=pl.ANY)
    return pl.pallas_call(
        pair_kernel,
        out_shape=(
            jax.ShapeDtypeStruct((4, 2 * L, WIN), BF),
            jax.ShapeDtypeStruct((4, 2 * L, WIN), BF),
            jax.ShapeDtypeStruct((2 * L, D), BF),
            jax.ShapeDtypeStruct((40, D), BF),
            jax.ShapeDtypeStruct((1, 2 * D), BF),
        ),
        in_specs=[smem, smem, smem, vmem, vmem, hbm, hbm, hbm, hbm],
        out_specs=(vmem,) * 5,
        scratch_shapes=[pltpu.VMEM((D, D), BF)] * 4
        + [
            pltpu.VMEM((2 * L, D), BF),
            pltpu.VMEM((2 * L, D), BF),
            pltpu.VMEM((2 * HEADS, L, L), F32),
            pltpu.VMEM((2 * HEADS, L), F32),
            pltpu.VMEM((2 * HEADS, L), F32),
            pltpu.VMEM((2 * L, D), F32),
            pltpu.VMEM((2 * L, D), F32),
            pltpu.VMEM((2 * L, D), BF),
            pltpu.VMEM((2 * L, D), BF),
            pltpu.SemaphoreType.DMA((4,)),
        ],
        compiler_params=pltpu.CompilerParams(vmem_limit_bytes=40 * 1024 * 1024),
        cost_estimate=pl.CostEstimate(
            flops=12 * 10**9, bytes_accessed=18 * 10**6, transcendentals=6 * 10**5
        ),
        name="pair_step",
    )(lengths, pairs, label, x, wc, wq, wk, wv, wo)


def grads_kernel(*refs):
    xs, ms, zp, out = refs[:8], refs[8:12], refs[12], refs[13]
    for r in range(5):
        cols = slice(256 * r, 256 * r + 256)
        acc = None
        for n in range(4):
            for c in range(2):
                term = mm(xs[2 * n + c][:, cols], ms[n][c], TN)
                acc = term if acc is None else acc + term
        out[:, WIN * r : WIN * r + WIN] = acc.astype(BF)
    acc = None
    for r in range(5):
        place = iota((40, 256), 1) == iota((40, 256), 0) + 40 * r
        term = mm(zp[:, 256 * r : 256 * r + 256], jnp.where(place, 1.0, 0.0).astype(BF), TN)
        acc = term if acc is None else acc + term
    out[:, 5 * WIN :] = acc.astype(BF)


def grads_step(xs, ms, zp):
    vmem = pl.BlockSpec(memory_space=pltpu.VMEM)
    return pl.pallas_call(
        grads_kernel,
        out_shape=jax.ShapeDtypeStruct((2 * L, 5 * WIN + 256), BF),
        in_specs=[vmem] * 13,
        out_specs=vmem,
        compiler_params=pltpu.CompilerParams(vmem_limit_bytes=24 * 1024 * 1024),
        cost_estimate=pl.CostEstimate(
            flops=2 * 10**9, bytes_accessed=9 * 10**6, transcendentals=0
        ),
        name="grads_step",
    )(*xs, *ms, zp)


def final_kernel(got, dv, wo, emb, out):
    to = iota((L, 2 * L), 0)
    frm = iota((L, 2 * L), 1)
    picks = [jnp.where(frm == 2 * to + c, 1.0, 0.0).astype(BF) for c in range(2)]
    for c in range(2):
        emb[c] = mm(picks[c], got[:, 0:D])
    kind = iota((HEADS, 2 * L), 0)
    src = iota((HEADS, 2 * L), 1)
    fold = jnp.where((src & 15) == kind, 1.0, 0.0).astype(BF)
    sums = mm(fold, got[:, D : D + 5 * WIN])
    lane = iota((1, 128), 1)
    for half in range(2):
        for r in range(5):
            i = 5 * half + r
            for m in range(2):
                wins = []
                for y in range(4):
                    row = 4 * y + 2 * m + half
                    wins.append(sums[row : row + 1, WIN * r : WIN * r + WIN])
                for pair in range(2):
                    left, right = wins[2 * pair], wins[2 * pair + 1]
                    join = jnp.where(lane < 64, left[:, 256:384], right[:, 0:128])
                    line = jnp.concatenate([left[:, 0:256], join, right[:, 128:384]], axis=1)
                    out[i, m : m + 1, 640 * pair : 640 * pair + 640] = line
    head_lane = iota((HEADS, D), 1)
    head_row = iota((HEADS, D), 0)
    headmask = (head_lane >= HD * head_row) & (head_lane < HD * head_row + HD)
    ext = got[:, D + 5 * WIN :]
    dvs = [dv[:, D * a : D * a + D] for a in range(2)]
    gs = [mm(d, wo[...], NT).astype(BF) for d in dvs]
    for half in range(2):
        e = mm(picks[half], ext).astype(BF)
        by_g = [mm(e, gs[a], TN) for a in range(2)]
        by_d = [mm(e, dvs[a], TN) for a in range(2)]
        for r in range(5):
            i = 5 * half + r
            base = 40 * r
            val = sum(
                jnp.where(headmask, by_g[a][base + 16 * a : base + 16 * a + 16, :], 0.0)
                for a in range(2)
            )
            out[i, 2:3, :] = jnp.sum(val, axis=0, keepdims=True)
            out[i, 3:4, :] = (
                by_d[0][base + 32 : base + 33, :] + by_d[1][base + 33 : base + 34, :]
            )


def final_step(got, dv, wo):
    vmem = pl.BlockSpec(memory_space=pltpu.VMEM)
    return pl.pallas_call(
        final_kernel,
        out_shape=(
            jax.ShapeDtypeStruct((2, L, D), F32),
            jax.ShapeDtypeStruct((10, 4, D), F32),
        ),
        in_specs=[vmem] * 3,
        out_specs=(vmem, vmem),
        compiler_params=pltpu.CompilerParams(vmem_limit_bytes=32 * 1024 * 1024),
        cost_estimate=pl.CostEstimate(
            flops=2 * 10**9, bytes_accessed=7 * 10**6, transcendentals=0
        ),
        name="final_step",
    )(got, dv, wo)


def swap_cores(a):
    return lax.ppermute(a, "dev", [(d, d ^ 1) for d in range(NDEV)])


def shift_y(a, step):
    route = []
    for d in range(NDEV):
        y = (d >> 1) & 3
        route.append((d, (d & ~6) | (((y + step) & 3) << 1)))
    return lax.ppermute(a, "dev", route)


def exchange(a):
    got = lax.all_to_all(a.reshape(NDEV, 2, a.shape[1]), "dev", 0, 0, tiled=True)
    return got


def shards(embeddings, lengths, pairs, labels, w_query, w_key, w_value, w_out, w_class):
    dev = lax.axis_index("dev")
    y = (dev >> 1) & 3
    ids = pairs.reshape(-1)
    select = (ids[:, None] == jnp.arange(2 * NDEV, dtype=jnp.int32)[None, :]).astype(BF)
    f = iota((D, D), 0)
    to = iota((D, D), 1)
    regroup = (f == 5 * (to & 255) + (to >> 8)).astype(BF)

    spread = lax.all_to_all(embeddings.transpose(1, 0, 2), "dev", 0, 0, tiled=True)
    picked = mm(select, spread.reshape(2 * NDEV, D)).astype(BF)
    x = exchange(picked).transpose(1, 0, 2).reshape(2 * L, D)

    xp = mm(x, regroup).astype(BF)
    xs = []
    for step in range(4):
        near = xp if step == 0 else shift_y(xp, step)
        xs += [near, swap_cores(near)]

    mine, other, dx, z, dv = pair_step(
        lengths, ids, labels, x, w_class.reshape(1, D), w_query, w_key, w_value, w_out
    )
    rows = exchange(dx).reshape(2 * NDEV, D)
    dv_all = lax.all_gather(dv, "dev", axis=0, tiled=True)

    both = jnp.stack([mine, swap_cores(other)], axis=1)
    ms = []
    for step in range(4):
        piece = lax.dynamic_index_in_dim(both, (y + step) & 3, 0, keepdims=False)
        ms.append(piece if step == 0 else shift_y(piece, step))
    zp = mm(z, regroup).astype(BF)
    tail = grads_step(xs, ms, zp)

    summed = mm(select, rows, TN).astype(BF)
    last = jnp.concatenate([summed, tail], axis=1)
    got = exchange(last).reshape(2 * NDEV, last.shape[1])
    return final_step(got, dv_all, w_out)


def solution(mesh):
    placed = (P("dev", None, None), P(), P(), P("dev"), P(), P(), P(), P(), P())
    return jax.shard_map(
        shards,
        mesh=mesh,
        in_specs=placed,
        out_specs=(P("dev", None, None), P("dev", None, None)),
        check_vma=False,
    )
```

time: 461 us -> 213 us (0.46); the launches traced: 454 us -> 213 us
  waiting for transfers between devices: 228 us -> 65.1 us
  local copies, waits for them, and re-layouts: 89.9 us -> 22.1 us
  matrix products: 38.1 us -> 4.8 us
  Pallas kernels: 0 us -> 26.2 us
  other arithmetic: 26.9 us -> 2.49 us
  blocking collectives: 30.9 us -> 52.4 us
  between operations: 16.1 us -> 1.53 us
  starting transfers between devices: 23.7 us -> 38.2 us
    unnamed x2 -> x0, waiting for transfers between devices: 175 us -> none
    all_gather x0 -> x1, blocking collectives: none -> 52.4 us  [shards(): dv_all = lax.all_gather(dv, 'dev', axis=0, tiled=True)]
    ppermute x0 -> x11, waiting for transfers between devices: none -> 36.2 us  [the longest x6 36.2 us: shift_y(): return lax.ppermute(a, 'dev', route)]
    dot_general x15 -> x4, matrix products: 38.1 us -> 4.8 us  [mm(): return lax.dot_general(a, b, dims, preferred_element_type=F32)]
    all_to_all x1 -> x0, blocking collectives: 30.9 us -> none  [shards(): lax.all_to_all(slot_grads, 'dev', split_axis=1, concat_axis=0, tiled=True)]
    reshape x9 -> x7, local copies, waits for them, and re-layouts: 40.5 us -> 10.7 us  [the longest x1 3.98 us: shards(): got = exchange(last).reshape(2 * NDEV, last.shape[1])]
    pallas_call x0 -> x3, Pallas kernels: none -> 26.2 us  [the longest x1 16.3 us: pair_step(): pl.pallas_call(pair_kernel, out_shape=(jax.ShapeDtypeStruct((4, 2 * L, WI...]
    all_to_all x3 -> x4, waiting for transfers between devices: 52.9 us -> 28.9 us  [the longest x1 14.6 us: shards(): lax.all_to_all(embeddings.transpose(1, 0, 2), 'dev', 0, 0, tiled=True)]
  transfers between devices with their start and end apart: 4 -> 15, of which waited for: 4 -> 5; matrix products, arithmetic and copies ran while one was open for 4% -> 5% of each run, Pallas kernels for 0% -> 0%
where the time goes in v1:
time: 213 us
  waiting for transfers between devices  65.1 us (31%)
  blocking collectives  52.4 us (25%)
  starting transfers between devices  38.2 us (18%)
  Pallas kernels  26.2 us (12%)
  local copies, waits for them, and re-layouts  22.1 us (10%)
  matrix products  4.8 us (2%)
  other arithmetic  2.49 us (1%)
    all_gather x1, blocking collectives, shards(): dv_all = lax.all_gather(dv, 'dev', axis=0, tiled=True)  52.4 us
    ppermute x6, waiting for transfers between devices, shift_y(): return lax.ppermute(a, 'dev', route)  36.2 us
    all_to_all x3, starting transfers between devices, exchange(): lax.all_to_all(a.reshape(NDEV, 2, a.shape[1]), 'dev', 0, 0, tiled=True)  16.8 us
    pallas_call x1, Pallas kernels, pair_step(): pl.pallas_call(pair_kernel, out_shape=(jax.ShapeDtypeStruct((4, 2 * L, WI...  16.3 us
    all_to_all x1, waiting for transfers between devices, shards(): lax.all_to_all(embeddings.transpose(1, 0, 2), 'dev', 0, 0, tiled=True)  14.6 us
    all_to_all x3, waiting for transfers between devices, exchange(): lax.all_to_all(a.reshape(NDEV, 2, a.shape[1]), 'dev', 0, 0, tiled=True)  14.3 us
    all_to_all x1, starting transfers between devices, shards(): lax.all_to_all(embeddings.transpose(1, 0, 2), 'dev', 0, 0, tiled=True)  11.5 us
    unnamed x25, local copies, waits for them, and re-layouts  11.1 us
  transfers between devices with their start and end apart: 15, of which 5 were waited for; matrix products, arithmetic and copies ran while one was open for 5% of the time, Pallas kernels for 0%

profile of v1, /device:TPU:1, one launch (start us, length us, event | category | flops | bytes accessed | tf_op | source)
XLA Modules:
  0.0 212.8 jit_solution(813190471426739150)
XLA Ops:
  0.6 2.6 %copy.25 = bf16[2,128,1280]{2,0,1:T(2,128)(2,1)} copy(bf16[2,128,1280]{2,1,0:T(8,128)(2,1)} %param.9) | data formatting | bytes 1310720 | tf_op args[0]
  3.2 11.5 %all-to-all-start = ((bf16[128,2,1280]{2,1,0:T(2,128)(2,1)}), bf16[128,2,1280]{2,1,0:T(2,128)(2,1)S(1)}, u32[]{:S(2)}, u32[]{:S(2)}) async-start(bf16[128,2,1280]{2,1,0:T(2,128)(2,1)} %bitcast.22), calls=%async_computation | async-start | bytes 1310720 | tf_op jit(solution)/shard_map/all_to_all | solution.py:341
  15.0 14.6 %all-to-all-done = bf16[128,2,1280]{2,1,0:T(2,128)(2,1)S(1)} async-done(((bf16[128,2,1280]{2,1,0:T(2,128)(2,1)}), bf16[128,2,1280]{2,1,0:T(2,128)(2,1)S(1)}, u32[]{:S(2)}, u32[]{:S(2)}) %all-to-all-start) | async-done | bytes 655392 | tf_op jit(solution)/shard_map/all_to_all | solution.py:341
  31.4 4.8 %all-to-all-start.1 = ((bf16[128,2,1280]{2,1,0:T(2,128)(2,1)}), bf16[128,2,1280]{2,1,0:T(2,128)(2,1)S(1)}, u32[]{:S(2)}, u32[]{:S(2)}) async-start(bf16[128,2,1280]{2,1,0:T(2,128)(2,1)} %reshape.31), calls=%async_computation.1 | async-start | bytes 1310720 | tf_op jit(solution)/shard_map/all_to_all | solution.py:328
  36.8 14.3 %all-to-all-done.1 = bf16[128,2,1280]{2,1,0:T(2,128)(2,1)S(1)} async-done(((bf16[128,2,1280]{2,1,0:T(2,128)(2,1)}), bf16[128,2,1280]{2,1,0:T(2,128)(2,1)S(1)}, u32[]{:S(2)}, u32[]{:S(2)}) %all-to-all-start.1) | async-done | bytes 655392 | tf_op jit(solution)/shard_map/all_to_all | solution.py:328
  51.2 1.9 copy-done
  53.1 1.9 copy-done.1
  55.0 1.9 copy-done.2
  57.0 16.3 %pair_step.1 = (bf16[4,256,384]{2,1,0:T(8,128)(2,1)S(1)}, bf16[4,256,384]{2,1,0:T(8,128)(2,1)}, bf16[256,1280]{1,0:T(8,128)(2,1)S(1)}, bf16[40,1280]{1,0:T(8,128)(2,1)S(1)}, bf16[1,2560]{1,0:T(2,128)(2,1)S(1)}) custom-call(s32[256]{0:T(256)S(1)} %copy-done.4, s32[256]{0:T(256)S(1)} %eq.20.pairs, s32[1]{0:T(128)S(6)} %copy.26.label, ...), custom_call_target="tpu_custom_call" | custom-call | flops 12000000000 | bytes 18000000 | tf_op jit(solution)/shard_map/pair_step/pallas_call | solution.py:185
  81.1 5.3 %all-to-all-start.2 = ((bf16[128,2,1280]{2,1,0:T(2,128)(2,1)}), bf16[128,2,1280]{2,1,0:T(2,128)(2,1)}, u32[]{:S(2)}, u32[]{:S(2)}) async-start(bf16[128,2,1280]{2,1,0:T(2,128)(2,1)} %reshape.34), calls=%async_computation.2 | async-start | bytes 1310720 | tf_op jit(solution)/shard_map/all_to_all | solution.py:328
  86.4 2.4 %fusion.7 = (bf16[2,256,384]{2,1,0:T(8,128)(2,1)S(1)}, bf16[2,256,384]{2,1,0:T(8,128)(2,1)S(1)}, bf16[2,256,384]{2,1,0:T(8,128)(2,1)}, bf16[2,256,384]{2,1,0:T(8,128)(2,1)}) fusion(s32[]{:T(128)S(6)} %select_n.16, bf16[4,1,256,384]{3,2,0,1:T(8,128)(2,1)S(1)} %bitcast.23, bf16[4,1,256,384]{3,2,0,1:T(8,128)(2,1)} %bitcast.4, s32[]{:T(128)S(6)} %select_n.13, ...), kind=kLoop, calls=%fused_computation.21 | loop fusion | flops 786432 | bytes 3145744 | tf_op jit(solution)/shard_map/jit(dynamic_index_in_dim)/squeeze | solution.py:360
  88.8 2.6 %collective-permute-start.10 = (bf16[2,256,384]{2,1,0:T(8,128)(2,1)S(1)}, bf16[2,256,384]{2,1,0:T(8,128)(2,1)S(1)}, u32[]{:S(2)}, u32[]{:S(2)}) collective-permute-start(bf16[2,256,384]{2,1,0:T(8,128)(2,1)S(1)} %get-tuple-element.12), channel_id=1, source_target_pairs={{0,6},{1,7},{2,0},{3,1},{4,2},{5,3},{6,4},{7,5},{8,14},{9,15},{10,... | collective-permute-start | bytes 1179656 | tf_op jit(solution)/shard_map/ppermute | solution.py:324
  91.4 22.9 %collective-permute-done.1.refs_2_ = bf16[256,1280]{1,0:T(8,128)(2,1)S(1)} collective-permute-done((bf16[256,1280]{1,0:T(8,128)(2,1)S(1)}, bf16[256,1280]{1,0:T(8,128)(2,1)S(1)}, u32[]{:S(2)}, u32[]{:S(2)}) %collective-permute-start.1) | collective-permute-done | bytes 655392 | tf_op jit(solution)/shard_map/ppermute | solution.py:324
  116.2 8.0 %collective-permute-done.10.refs_11_ = bf16[2,256,384]{2,1,0:T(8,128)(2,1)S(1)} collective-permute-done((bf16[2,256,384]{2,1,0:T(8,128)(2,1)S(1)}, bf16[2,256,384]{2,1,0:T(8,128)(2,1)S(1)}, u32[]{:S(2)}, u32[]{:S(2)}) %collective-permute-start.10) | collective-permute-done | bytes 393248 | tf_op jit(solution)/shard_map/ppermute | solution.py:324
  126.3 2.7 %reshape.35 = bf16[256,1280]{1,0:T(8,128)(2,1)} reshape(bf16[128,2,1280]{2,1,0:T(2,128)(2,1)} %all-to-all-done.2) | data formatting | bytes 1310720 | tf_op jit(solution)/shard_map/reshape | solution.py:354
  129.1 1.6 convolution_convert_fusion
  130.7 5.2 %collective-permute-done.9.refs_10_ = bf16[2,256,384]{2,1,0:T(8,128)(2,1)} collective-permute-done((bf16[2,256,384]{2,1,0:T(8,128)(2,1)}, bf16[2,256,384]{2,1,0:T(8,128)(2,1)}, u32[]{:S(2)}, u32[]{:S(2)}) %collective-permute-start.9) | collective-permute-done | bytes 393248 | tf_op jit(solution)/shard_map/ppermute | solution.py:324
  135.9 5.0 %grads_step.1 = bf16[256,2176]{1,0:T(8,128)(2,1)S(1)} custom-call(bf16[256,1280]{1,0:T(8,128)(2,1)S(1)} %fusion.4.refs_0_, bf16[256,1280]{1,0:T(8,128)(2,1)} %collective-permute-done.refs_1_, bf16[256,1280]{1,0:T(8,128)(2,1)S(1)} %collective-permute-done.1.refs_2_, bf16[256,1280]{1,0:T(8,128)(2,1)S(1)} %collective-permute-done.2.refs_3_, ...), custom_call_target="tpu_custom_call" | custom-call | flops 2000000000 | bytes 9000000 | tf_op jit(solution)/shard_map/grads_step/pallas_call | solution.py:237
  141.0 1.6 reshape.36
  142.6 6.8 %all-to-all-start.3 = ((bf16[128,2,3456]{2,1,0:T(2,128)(2,1)}), bf16[128,2,3456]{2,1,0:T(2,128)(2,1)}, u32[]{:S(2)}, u32[]{:S(2)}) async-start(bf16[128,2,3456]{2,1,0:T(2,128)(2,1)} %reshape.36), calls=%async_computation.3 | async-start | bytes 3538944 | tf_op jit(solution)/shard_map/all_to_all | solution.py:328
  149.4 52.4 %all-gather = bf16[128,1,2560]{2,1,0:T(2,128)(2,1)S(1)} all-gather(bf16[1,1,2560]{2,1,0:T(2,128)(2,1)S(1)} %bitcast.27), channel_id=1, replica_groups=mesh['dev'=128] {'dev'}, dimensions={0}, use_global_device_ids=true | all-gather | bytes 660480 | tf_op jit(solution)/shard_map/all_gather | solution.py:355
  201.9 4.0 %reshape.37.got = bf16[256,3456]{1,0:T(8,128)(2,1)S(1)} reshape(bf16[128,2,3456]{2,1,0:T(2,128)(2,1)} %all-to-all-done.3) | data formatting | bytes 3538944 | tf_op jit(solution)/shard_map/reshape | solution.py:367
  205.9 1.9 copy-done.3
  207.8 4.9 %final_step.1 = (f32[2,128,1280]{2,1,0:T(8,128)}, f32[10,4,1280]{2,1,0:T(4,128)}) custom-call(bf16[256,3456]{1,0:T(8,128)(2,1)S(1)} %reshape.37.got, bf16[128,2560]{1,0:T(8,128)(2,1)S(1)} %bitcast.26, bf16[1280,1280]{1,0:T(8,128)(2,1)S(1)} %copy-done.3), custom_call_target="tpu_custom_call" | custom-call | flops 2000000000 | bytes 7000000 | tf_op jit(solution)/shard_map/final_step/pallas_call | solution.py:299
  (51 shorter events, 14.1 us)
Async XLA Ops:
  0.6 14.1 %copy-start.10 = (s32[128,2]{0,1:T(2,128)S(1)}, s32[128,2]{0,1:T(2,128)}, u32[]{:S(2)}) copy-start(s32[128,2]{0,1:T(2,128)} %param.11) | copy-start | bytes 3076
  3.2 26.4 %all-to-all-start = ((bf16[128,2,1280]{2,1,0:T(2,128)(2,1)}), bf16[128,2,1280]{2,1,0:T(2,128)(2,1)S(1)}, u32[]{:S(2)}, u32[]{:S(2)}) async-start(bf16[128,2,1280]{2,1,0:T(2,128)(2,1)} %bitcast.22), calls=%async_computation | async-start | bytes 1310720 | tf_op jit(solution)/shard_map/all_to_all | solution.py:341
  30.3 5.9 %copy-start.9 = (f32[1280]{0:T(1024)S(1)}, f32[1280]{0:T(1024)}, u32[]{:S(2)}) copy-start(f32[1280]{0:T(1024)} %param.17) | copy-start | bytes 15364
  31.4 19.8 %copy-start.4 = (s32[256]{0:T(256)S(1)}, s32[256]{0:T(256)}, u32[]{:S(2)}) copy-start(s32[256]{0:T(256)} %lengths.1) | copy-start | bytes 3076
  31.4 19.7 %all-to-all-start.1 = ((bf16[128,2,1280]{2,1,0:T(2,128)(2,1)}), bf16[128,2,1280]{2,1,0:T(2,128)(2,1)S(1)}, u32[]{:S(2)}, u32[]{:S(2)}) async-start(bf16[128,2,1280]{2,1,0:T(2,128)(2,1)} %reshape.31), calls=%async_computation.1 | async-start | bytes 1310720 | tf_op jit(solution)/shard_map/all_to_all | solution.py:328
  51.2 1.9 copy-start
  53.1 1.9 copy-start.1
  73.3 3.3 %copy-start.5 = (bf16[40,1280]{1,0:T(8,128)(2,1)}, bf16[40,1280]{1,0:T(8,128)(2,1)S(1)}, u32[]{:S(2)}) copy-start(bf16[40,1280]{1,0:T(8,128)(2,1)S(1)} %get-tuple-element.10) | copy-start | bytes 307204
  73.3 13.1 %collective-permute-start.7 = (bf16[4,256,384]{2,1,0:T(8,128)(2,1)}, bf16[4,256,384]{2,1,0:T(8,128)(2,1)}, u32[]{:S(2)}, u32[]{:S(2)}) collective-permute-start(bf16[4,256,384]{2,1,0:T(8,128)(2,1)} %get-tuple-element.9), channel_id=1, source_target_pairs={{0,1},{1,0},{2,3},{3,2},{4,5},{5,4},{6,7},{7,6},{8,9},{9,8},{10,11... | collective-permute-start | bytes 2359304 | tf_op jit(solution)/shard_map/ppermute | solution.py:316
  76.6 37.8 %collective-permute-start.1 = (bf16[256,1280]{1,0:T(8,128)(2,1)S(1)}, bf16[256,1280]{1,0:T(8,128)(2,1)S(1)}, u32[]{:S(2)}, u32[]{:S(2)}) collective-permute-start(bf16[256,1280]{1,0:T(8,128)(2,1)S(1)} %fusion.4.refs_0_), channel_id=1, source_target_pairs={{0,2},{1,3},{2,4},{3,5},{4,6},{5,7},{6,0},{7,1},{8,10},{9,11},{10,... | collective-permute-start | bytes 1966088 | tf_op jit(solution)/shard_map/ppermute | solution.py:324
  76.8 38.8 %collective-permute-start.3 = (bf16[256,1280]{1,0:T(8,128)(2,1)S(1)}, bf16[256,1280]{1,0:T(8,128)(2,1)S(1)}, u32[]{:S(2)}, u32[]{:S(2)}) collective-permute-start(bf16[256,1280]{1,0:T(8,128)(2,1)S(1)} %fusion.4.refs_0_), channel_id=1, source_target_pairs={{0,4},{1,5},{2,6},{3,7},{4,0},{5,1},{6,2},{7,3},{8,12},{9,13},{10,... | collective-permute-start | bytes 1966088 | tf_op jit(solution)/shard_map/ppermute | solution.py:324
  78.3 37.3 %collective-permute-start.5 = (bf16[256,1280]{1,0:T(8,128)(2,1)S(1)}, bf16[256,1280]{1,0:T(8,128)(2,1)}, u32[]{:S(2)}, u32[]{:S(2)}) collective-permute-start(bf16[256,1280]{1,0:T(8,128)(2,1)S(1)} %fusion.4.refs_0_), channel_id=1, source_target_pairs={{0,6},{1,7},{2,0},{3,1},{4,2},{5,3},{6,4},{7,5},{8,14},{9,15},{10,... | collective-permute-start | bytes 1966088 | tf_op jit(solution)/shard_map/ppermute | solution.py:324
  79.4 36.8 %collective-permute-start = (bf16[256,1280]{1,0:T(8,128)(2,1)S(1)}, bf16[256,1280]{1,0:T(8,128)(2,1)}, u32[]{:S(2)}, u32[]{:S(2)}) collective-permute-start(bf16[256,1280]{1,0:T(8,128)(2,1)S(1)} %fusion.4.refs_0_), channel_id=1, source_target_pairs={{0,1},{1,0},{2,3},{3,2},{4,5},{5,4},{6,7},{7,6},{8,9},{9,8},{10,11... | collective-permute-start | bytes 1966088 | tf_op jit(solution)/shard_map/ppermute | solution.py:316
  81.1 45.2 %all-to-all-start.2 = ((bf16[128,2,1280]{2,1,0:T(2,128)(2,1)}), bf16[128,2,1280]{2,1,0:T(2,128)(2,1)}, u32[]{:S(2)}, u32[]{:S(2)}) async-start(bf16[128,2,1280]{2,1,0:T(2,128)(2,1)} %reshape.34), calls=%async_computation.2 | async-start | bytes 1310720 | tf_op jit(solution)/shard_map/all_to_all | solution.py:328
  86.4 38.6 %copy-start.6 = (bf16[40,1280]{1,0:T(8,128)(2,1)S(1)}, bf16[40,1280]{1,0:T(8,128)(2,1)}, u32[]{:S(2)}) copy-start(bf16[40,1280]{1,0:T(8,128)(2,1)} %copy-done.5) | copy-start | bytes 307204
  86.4 38.6 %copy-start.8 = (s32[1280]{0:T(1024)S(1)}, s32[1280]{0:T(1024)}, u32[]{:S(2)}) copy-start(s32[1280]{0:T(1024)} %copy-done.7) | copy-start | bytes 15364
  88.8 35.4 %collective-permute-start.10 = (bf16[2,256,384]{2,1,0:T(8,128)(2,1)S(1)}, bf16[2,256,384]{2,1,0:T(8,128)(2,1)S(1)}, u32[]{:S(2)}, u32[]{:S(2)}) collective-permute-start(bf16[2,256,384]{2,1,0:T(8,128)(2,1)S(1)} %get-tuple-element.12), channel_id=1, source_target_pairs={{0,6},{1,7},{2,0},{3,1},{4,2},{5,3},{6,4},{7,5},{8,14},{9,15},{10,... | collective-permute-start | bytes 1179656 | tf_op jit(solution)/shard_map/ppermute | solution.py:324
  114.4 21.5 %collective-permute-start.2 = (bf16[256,1280]{1,0:T(8,128)(2,1)S(1)}, bf16[256,1280]{1,0:T(8,128)(2,1)S(1)}, u32[]{:S(2)}, u32[]{:S(2)}) collective-permute-start(bf16[256,1280]{1,0:T(8,128)(2,1)S(1)} %collective-permute-done.1.refs_2_), channel_id=1, source_target_pairs={{0,1},{1,0},{2,3},{3,2},{4,5},{5,4},{6,7},{7,6},{8,9},{9,8},{10,11... | collective-permute-start | bytes 1966088 | tf_op jit(solution)/shard_map/ppermute | solution.py:316
  115.6 20.2 %collective-permute-start.4 = (bf16[256,1280]{1,0:T(8,128)(2,1)S(1)}, bf16[256,1280]{1,0:T(8,128)(2,1)}, u32[]{:S(2)}, u32[]{:S(2)}) collective-permute-start(bf16[256,1280]{1,0:T(8,128)(2,1)S(1)} %collective-permute-done.3.refs_4_), channel_id=1, source_target_pairs={{0,1},{1,0},{2,3},{3,2},{4,5},{5,4},{6,7},{7,6},{8,9},{9,8},{10,11... | collective-permute-start | bytes 1966088 | tf_op jit(solution)/shard_map/ppermute | solution.py:316
  115.7 20.2 %collective-permute-start.6 = (bf16[256,1280]{1,0:T(8,128)(2,1)}, bf16[256,1280]{1,0:T(8,128)(2,1)}, u32[]{:S(2)}, u32[]{:S(2)}) collective-permute-start(bf16[256,1280]{1,0:T(8,128)(2,1)} %collective-permute-done.5.refs_6_), channel_id=1, source_target_pairs={{0,1},{1,0},{2,3},{3,2},{4,5},{5,4},{6,7},{7,6},{8,9},{9,8},{10,11... | collective-permute-start | bytes 1966088 | tf_op jit(solution)/shard_map/ppermute | solution.py:316
  116.2 14.5 %collective-permute-start.8 = (bf16[2,256,384]{2,1,0:T(8,128)(2,1)}, bf16[2,256,384]{2,1,0:T(8,128)(2,1)}, u32[]{:S(2)}, u32[]{:S(2)}) collective-permute-start(bf16[2,256,384]{2,1,0:T(8,128)(2,1)} %get-tuple-element.14), channel_id=1, source_target_pairs={{0,2},{1,3},{2,4},{3,5},{4,6},{5,7},{6,0},{7,1},{8,10},{9,11},{10,... | collective-permute-start | bytes 1179656 | tf_op jit(solution)/shard_map/ppermute | solution.py:324
  124.2 11.7 %collective-permute-start.9 = (bf16[2,256,384]{2,1,0:T(8,128)(2,1)}, bf16[2,256,384]{2,1,0:T(8,128)(2,1)}, u32[]{:S(2)}, u32[]{:S(2)}) collective-permute-start(bf16[2,256,384]{2,1,0:T(8,128)(2,1)} %get-tuple-element.15), channel_id=1, source_target_pairs={{0,4},{1,5},{2,6},{3,7},{4,0},{5,1},{6,2},{7,3},{8,12},{9,13},{10,... | collective-permute-start | bytes 1179656 | tf_op jit(solution)/shard_map/ppermute | solution.py:324
  142.6 59.3 %all-to-all-start.3 = ((bf16[128,2,3456]{2,1,0:T(2,128)(2,1)}), bf16[128,2,3456]{2,1,0:T(2,128)(2,1)}, u32[]{:S(2)}, u32[]{:S(2)}) async-start(bf16[128,2,3456]{2,1,0:T(2,128)(2,1)} %reshape.36), calls=%async_computation.3 | async-start | bytes 3538944 | tf_op jit(solution)/shard_map/all_to_all | solution.py:328
  205.9 1.9 copy-start.3
  (2 other events, 2.5 us)

commit v2 on v1

v2 whole, which is shorter than its diff:
```python
import functools

import jax
import jax.numpy as jnp
from jax import lax
from jax.experimental import pallas as pl
from jax.experimental.pallas import tpu as pltpu
from jax.sharding import PartitionSpec as P

HEADS = 16
HD = 80
L = 128
D = 1280
NDEV = 128
HALF = 640
BF = jnp.bfloat16
F32 = jnp.float32
NN = (((1,), (0,)), ((), ()))
NT = (((1,), (1,)), ((), ()))
TN = (((0,), (0,)), ((), ()))


def mm(a, b, dims=NN):
    return lax.dot_general(a, b, dims, preferred_element_type=F32)


def iota(shape, dim):
    return lax.broadcasted_iota(jnp.int32, shape, dim)


def split(a):
    hi = a.astype(BF)
    return hi, (a - hi.astype(F32)).astype(BF)


def pair_kernel(
    lengths, pairs, label, x_h, wc, wq_h, wk_h, wv_h, wo_h,
    *refs,
):
    pieces_h, (dx_h, z) = refs[:4], refs[4:6]
    x, wq, wk, wv, wo, q, k, p, s, u, dqk, dqb, dkb, back, woven, pieces, dx, sems, out_sems = refs[6:]
    dev = lax.axis_index("dev")
    loads = []
    for n, (src, dst) in enumerate(((x_h, x), (wq_h, wq), (wk_h, wk), (wv_h, wv), (wo_h, wo))):
        load = pltpu.make_async_copy(src, dst, sems.at[n])
        load.start()
        loads.append(load)
    lens = [lengths[pairs[2 * dev]], lengths[pairs[2 * dev + 1]]]
    rows = iota((L, L), 0)
    lanes = iota((L, L), 1)
    scale = HD ** (-0.5)

    loads[0].wait()
    loads[1].wait()
    for n in range(5):
        cols = slice(256 * n, 256 * n + 256)
        q[:, cols] = mm(x[...], wq[:, cols]).astype(BF)
    loads[2].wait()
    for n in range(5):
        cols = slice(256 * n, 256 * n + 256)
        k[:, cols] = mm(x[...], wk[:, cols]).astype(BF)

    spans = []
    for h in range(HEADS):
        low = HD * h
        first = low // 128 * 128
        last = (low + HD - 1) // 128 * 128 + 128
        spans.append((low, first, last))

    for h, (low, first, last) in enumerate(spans):
        lane = iota((L, last - first), 1) + first
        inside = jnp.where((lane >= low) & (lane < low + HD), 1.0, 0.0).astype(BF)
        for a in range(2):
            b = 1 - a
            qt = q[L * a : L * a + L, first:last] * inside
            scores = mm(qt, k[L * b : L * b + L, first:last], NT) * scale
            scores = jnp.where(lanes < lens[b], scores, -1000000000.0)
            expo = jnp.exp(scores - jnp.max(scores, axis=1, keepdims=True))
            prob = expo / jnp.sum(expo, axis=1, keepdims=True)
            prob = jnp.where(rows < lens[a], prob, 0.0)
            p[a * HEADS + h] = prob
            s[a * HEADS + h : a * HEADS + h + 1, :] = jnp.sum(
                prob.astype(BF).astype(F32), axis=0, keepdims=True
            )

    head_lane = iota((HEADS, D), 1)
    head_row = iota((HEADS, D), 0)
    headmask = (head_lane >= HD * head_row) & (head_lane < HD * head_row + HD)
    ys = []
    for a in range(2):
        b = 1 - a
        hi, lo = split(s[a * HEADS : a * HEADS + HEADS, :])
        ys.append(mm(hi, x[L * b : L * b + L, :]) + mm(lo, x[L * b : L * b + L, :]))
    y = jnp.concatenate(ys, axis=0)
    y_hi, y_lo = split(y)
    loads[3].wait()
    t = mm(y_hi, wv[...]) + mm(y_lo, wv[...])
    pooled_ctx = [
        jnp.sum(jnp.where(headmask, t[HEADS * a : HEADS * a + HEADS, :], 0.0), axis=0, keepdims=True)
        for a in range(2)
    ]
    row8 = iota((8, D), 0)
    ctx8 = jnp.where(row8 == 0, pooled_ctx[0], jnp.where(row8 == 1, pooled_ctx[1], 0.0))
    z[...] = jnp.concatenate([y, ctx8], axis=0).astype(BF)
    mask_row = iota((8, 2 * L), 0)
    mask_lane = iota((8, 2 * L), 1)
    mask8 = ((mask_row == 0) & (mask_lane < lens[0])) | (
        (mask_row == 1) & (mask_lane >= L) & (mask_lane < L + lens[1])
    )
    x_sum = mm(jnp.where(mask8, 1.0, 0.0).astype(BF), x[...])
    ctx_hi, ctx_lo = split(ctx8)
    loads[4].wait()
    total = x_sum + mm(ctx_hi, wo[...]) + mm(ctx_lo, wo[...])
    lens_f = [n.astype(F32) for n in lens]
    pooled = [total[0:1, :] / lens_f[0], total[1:2, :] / lens_f[1]]
    logit = jnp.sum(wc[...] * pooled[0] * pooled[1], axis=1, keepdims=True)
    slope = 1.0 / (1.0 + jnp.exp(-logit)) - label[0].astype(F32)
    dvec = [slope * wc[...] * pooled[1 - a] / lens_f[a] for a in range(2)]
    dvec8 = jnp.where(row8 == 0, dvec[0], jnp.where(row8 == 1, dvec[1], 0.0)).astype(BF)
    g = mm(dvec8, wo[...], NT).astype(BF).astype(F32)
    gm = jnp.concatenate(
        [jnp.where(headmask, g[a : a + 1, :], 0.0) for a in range(2)], axis=0
    ).astype(BF)
    gv = mm(gm, wv[...], NT)
    gv_hi, gv_lo = split(gv)
    for a in range(2):
        b = 1 - a
        part = slice(HEADS * a, HEADS * a + HEADS)
        xb = x[L * b : L * b + L, :]
        u[part, :] = mm(gv_hi[part, :], xb, NT) + mm(gv_lo[part, :], xb, NT)

    for h, (low, first, last) in enumerate(spans):
        keep = lanes + first >= low
        for a in range(2):
            b = 1 - a
            row = a * HEADS + h
            prob = p[row]
            uh = u[row : row + 1, :]
            mean = jnp.sum(prob * uh, axis=1, keepdims=True)
            ds = (prob * (uh - mean) * scale).astype(BF)
            for out, side, val in (
                (0, a, mm(ds, k[L * b : L * b + L, first:last])),
                (1, b, mm(ds, q[L * a : L * a + L, first:last], TN)),
            ):
                here = slice(L * side, L * side + L)
                head = val[:, 0:128]
                if low > first:
                    head = jnp.where(keep, head, dqk[out, here, first : first + 128])
                dqk[out, here, first : first + 128] = head
                if last - first > 128:
                    dqk[out, here, first + 128 : last] = val[:, 128:]

    core = dev & 1
    side = (dev >> 1) & 1
    stores = []
    for n in range(4):
        start = pl.multiple_of((side ^ (n >> 1)) * HALF, 128)
        pieces[n] = dqk[core ^ (n & 1), :, pl.ds(start, HALF)].astype(BF)
        store = pltpu.make_async_copy(pieces.at[n], pieces_h[n], out_sems.at[n])
        store.start()
        stores.append(store)
    dqb[...] = dqk[0].astype(BF)
    dkb[...] = dqk[1].astype(BF)

    s_b = s[...].astype(BF)
    tall = iota((L, 256), 0)
    for n in range(5):
        cols = slice(256 * n, 256 * n + 256)
        acc = mm(dqb[...], wq[cols, :], NT) + mm(dkb[...], wk[cols, :], NT)
        for c in range(2):
            a = 1 - c
            part = slice(HEADS * a, HEADS * a + HEADS)
            val = acc[L * c : L * c + L, :] + mm(s_b[part, :], gv_hi[part, cols], TN)
            val = val + jnp.where(tall < lens[c], dvec[c][:, cols], 0.0)
            back[L * c : L * c + L, cols] = val
    for c in range(2):
        for half in range(2):
            row = 2 * c + half
            for n in range(5):
                cols = slice(HALF * half + L * n, HALF * half + L * n + L)
                woven[n, pl.ds(row, L, stride=8), :] = back[L * c : L * c + L, cols]
                woven[n, pl.ds(row + 4, L, stride=8), :] = jnp.broadcast_to(
                    dvec[c][:, cols], (L, L)
                )
    for n in range(4):
        part = slice(256 * n, 256 * n + 256)
        for m in range(5):
            dx[part, L * m : L * m + L] = woven[m, part, :].astype(BF)
        store = pltpu.make_async_copy(dx.at[part, :], dx_h.at[part, :], out_sems.at[4 + n])
        store.start()
        stores.append(store)
    for store in stores:
        store.wait()


def pair_step(lengths, pairs, label, x, wc, wq, wk, wv, wo):
    smem = pl.BlockSpec(memory_space=pltpu.SMEM)
    vmem = pl.BlockSpec(memory_space=pltpu.VMEM)
    hbm = pl.BlockSpec(memory_space=pl.ANY)
    return pl.pallas_call(
        pair_kernel,
        out_shape=(jax.ShapeDtypeStruct((2 * L, HALF), BF),) * 4
        + (
            jax.ShapeDtypeStruct((8 * L, HALF), BF),
            jax.ShapeDtypeStruct((40, D), BF),
        ),
        in_specs=[smem, smem, smem, hbm, vmem, hbm, hbm, hbm, hbm],
        out_specs=(hbm,) * 5 + (vmem,),
        scratch_shapes=[pltpu.VMEM((2 * L, D), BF)]
        + [pltpu.VMEM((D, D), BF)] * 4
        + [
            pltpu.VMEM((2 * L, D), BF),
            pltpu.VMEM((2 * L, D), BF),
            pltpu.VMEM((2 * HEADS, L, L), F32),
            pltpu.VMEM((2 * HEADS, L), F32),
            pltpu.VMEM((2 * HEADS, L), F32),
            pltpu.VMEM((2, 2 * L, D), F32),
            pltpu.VMEM((2 * L, D), BF),
            pltpu.VMEM((2 * L, D), BF),
            pltpu.VMEM((2 * L, D), F32),
            pltpu.VMEM((5, 8 * L, L), F32),
            pltpu.VMEM((4, 2 * L, HALF), BF),
            pltpu.VMEM((8 * L, HALF), BF),
            pltpu.SemaphoreType.DMA((5,)),
            pltpu.SemaphoreType.DMA((8,)),
        ],
        compiler_params=pltpu.CompilerParams(vmem_limit_bytes=60 * 1024 * 1024),
        cost_estimate=pl.CostEstimate(
            flops=12 * 10**9, bytes_accessed=18 * 10**6, transcendentals=6 * 10**5
        ),
        name="pair_step",
    )(lengths, pairs, label, x, wc, wq, wk, wv, wo)


def grads_kernel(*refs):
    ins, z, out_h = refs[:8], refs[8], refs[9]
    xs, ms, sums, zt, woven, out, sems, out_sems = refs[10:]
    loads = []
    for n in range(4):
        loads.append(pltpu.make_async_copy(ins[n], xs.at[n], sems.at[n]))
        loads.append(pltpu.make_async_copy(ins[4 + n], ms.at[n], sems.at[4 + n]))
    for load in loads:
        load.start()
    unit = jnp.where(iota((40, L), 0) == iota((40, L), 1), 1.0, 0.0).astype(BF)
    zt[...] = mm(z[...], unit, TN)
    for load in loads:
        load.wait()
    for n in range(5):
        cols = slice(256 * n, 256 * n + 256)
        acc = None
        for m in range(4):
            term = mm(xs[m, :, cols], ms[m], TN)
            acc = term if acc is None else acc + term
        for half in range(5):
            sums[half, cols, :] = acc[:, L * half : L * half + L]
    for i in range(10):
        pick = pl.ds(i, L, stride=10)
        for row in range(2):
            woven[i, pl.ds(row, L, stride=8), :] = jnp.zeros((L, L), F32)
        for n in range(5):
            woven[5 * (i % 2) + n, pl.ds(2 + i // 2, L, stride=8), :] = sums[n, pick, :]
        woven[i, pl.ds(7, L, stride=8), :] = zt[pick, :]
    stores = []
    for n in range(4):
        part = slice(256 * n, 256 * n + 256)
        for m in range(10):
            out[part, L * m : L * m + L] = woven[m, part, :].astype(BF)
        store = pltpu.make_async_copy(out.at[part, :], out_h.at[part, :], out_sems.at[n])
        store.start()
        stores.append(store)
    for store in stores:
        store.wait()


def grads_step(xs, ms, z):
    vmem = pl.BlockSpec(memory_space=pltpu.VMEM)
    hbm = pl.BlockSpec(memory_space=pl.ANY)
    return pl.pallas_call(
        grads_kernel,
        out_shape=jax.ShapeDtypeStruct((8 * L, D), BF),
        in_specs=[hbm] * 8 + [vmem],
        out_specs=hbm,
        scratch_shapes=[
            pltpu.VMEM((4, 2 * L, D), BF),
            pltpu.VMEM((4, 2 * L, HALF), BF),
            pltpu.VMEM((5, D, L), F32),
            pltpu.VMEM((D, L), F32),
            pltpu.VMEM((10, 8 * L, L), F32),
            pltpu.VMEM((8 * L, D), BF),
            pltpu.SemaphoreType.DMA((8,)),
            pltpu.SemaphoreType.DMA((4,)),
        ],
        compiler_params=pltpu.CompilerParams(vmem_limit_bytes=60 * 1024 * 1024),
        cost_estimate=pl.CostEstimate(
            flops=12 * 10**9, bytes_accessed=7 * 10**6, transcendentals=0
        ),
        name="grads_step",
    )(*xs, *ms, z)


def sum_kernel(rows_h, ids, tail_h, out_h, rows, tail, out, sems, out_sems):
    loads = []
    for n in range(4):
        part = (slice(256 * n, 256 * n + 256), slice(None))
        loads.append(pltpu.make_async_copy(rows_h.at[part], rows.at[part], sems.at[n]))
    for n in range(4):
        part = (slice(256 * n, 256 * n + 256), slice(None))
        loads.append(pltpu.make_async_copy(tail_h.at[part], tail.at[part], sems.at[4 + n]))
    for load in loads:
        load.start()
    chain = iota((2 * NDEV, 256), 0)
    halves = [None, None]
    for n in range(4):
        part = slice(256 * n, 256 * n + 256)
        loads[n].wait()
        for half in range(2):
            select = jnp.where(chain == ids[half : half + 1, part], 1.0, 0.0).astype(BF)
            term = mm(select, rows[part, :])
            halves[half] = term if n == 0 else halves[half] + term
    summed = jnp.concatenate(halves, axis=1).astype(BF)
    stores = []
    for n in range(4):
        part = slice(256 * n, 256 * n + 256)
        to = iota((256, 64), 0)
        frm = iota((256, 64), 1)
        weave = jnp.where(to == 8 * (frm >> 1) + (frm & 1), 1.0, 0.0).astype(BF)
        val = mm(weave, summed[64 * n : 64 * n + 64, :])
        loads[4 + n].wait()
        out[part, :] = (val + tail[part, :].astype(F32)).astype(BF)
        store = pltpu.make_async_copy(out.at[part, :], out_h.at[part, :], out_sems.at[n])
        store.start()
        stores.append(store)
    for store in stores:
        store.wait()


def sum_step(rows, ids, tail):
    vmem = pl.BlockSpec(memory_space=pltpu.VMEM)
    hbm = pl.BlockSpec(memory_space=pl.ANY)
    return pl.pallas_call(
        sum_kernel,
        out_shape=jax.ShapeDtypeStruct((8 * L, D), BF),
        in_specs=[hbm, vmem, hbm],
        out_specs=hbm,
        scratch_shapes=[
            pltpu.VMEM((8 * L, HALF), BF),
            pltpu.VMEM((8 * L, D), BF),
            pltpu.VMEM((8 * L, D), BF),
            pltpu.SemaphoreType.DMA((8,)),
            pltpu.SemaphoreType.DMA((4,)),
        ],
        compiler_params=pltpu.CompilerParams(vmem_limit_bytes=60 * 1024 * 1024),
        cost_estimate=pl.CostEstimate(
            flops=2 * 10**9, bytes_accessed=7 * 10**6, transcendentals=0
        ),
        name="sum_step",
    )(rows, ids, tail)


def vectors_kernel(rows, wo, dv, g):
    to = iota((2 * NDEV, 8 * L), 0)
    frm = iota((2 * NDEV, 8 * L), 1)
    for n in range(2):
        place = frm == 8 * (to & 127) + 4 + 2 * (to >> 7) + n
        pick = jnp.where(place, 1.0, 0.0).astype(BF)
        dv[:, HALF * n : HALF * n + HALF] = mm(pick, rows[...]).astype(BF)
    for n in range(5):
        cols = slice(256 * n, 256 * n + 256)
        g[:, cols] = mm(dv[...], wo[cols, :], NT).astype(BF)


def vectors_step(rows, wo):
    vmem = pl.BlockSpec(memory_space=pltpu.VMEM)
    return pl.pallas_call(
        vectors_kernel,
        out_shape=(jax.ShapeDtypeStruct((2 * NDEV, D), BF),) * 2,
        in_specs=[vmem] * 2,
        out_specs=(vmem,) * 2,
        compiler_params=pltpu.CompilerParams(vmem_limit_bytes=60 * 1024 * 1024),
        cost_estimate=pl.CostEstimate(
            flops=2 * 10**9, bytes_accessed=6 * 10**6, transcendentals=0
        ),
        name="vectors_step",
    )(rows, wo)


def final_kernel(got_h, dv_h, g_h, emb_h, out, got, dv, g, emb, wide, sums, sems, out_sems):
    loads = []
    for n in range(4):
        part = (slice(256 * n, 256 * n + 256), slice(None))
        loads.append(pltpu.make_async_copy(got_h.at[part], got.at[part], sems.at[n]))
    loads.append(pltpu.make_async_copy(dv_h, dv, sems.at[4]))
    loads.append(pltpu.make_async_copy(g_h, g, sems.at[5]))
    for load in loads:
        load.start()
    kind = iota((L, 256), 0)
    src = iota((L, 256), 1)
    t = src & 7
    same = (kind & 31) == (src >> 3)
    role = 4 * (t - 2) + ((src >> 3) & 3)
    want = ((kind < 64) & (t == (kind >> 5)) & same) | ((kind >= 64) & (kind < 96) & (t == 7) & same)
    want = want | ((kind >= 96) & (kind < 116) & (role == kind - 96))
    pick = jnp.where(want, 1.0, 0.0).astype(BF)
    stores = []
    for n in range(4):
        loads[n].wait()
        val = mm(pick, got[256 * n : 256 * n + 256, :])
        part = slice(32 * n, 32 * n + 32)
        for c in range(2):
            emb[c, part, :] = val[32 * c : 32 * c + 32, :]
            store = pltpu.make_async_copy(
                emb.at[c, part, :], emb_h.at[c, part, :], out_sems.at[2 * n + c]
            )
            store.start()
            stores.append(store)
        wide[part, :] = val[64:96, :].astype(BF)
        sums[...] = val[96:128, :] if n == 0 else sums[...] + val[96:128, :]
    ext = None
    for i in range(10):
        place = (iota((L, 512), 1) == iota((L, 512), 0) + 40 * i) & (iota((L, 512), 0) < 40)
        term = mm(wide[:, L * i : L * i + L], jnp.where(place, 1.0, 0.0).astype(BF))
        ext = term if ext is None else ext + term
    ext = ext.astype(BF)
    loads[4].wait()
    loads[5].wait()
    head_lane = iota((HEADS, D), 1)
    head_row = iota((HEADS, D), 0)
    headmask = (head_lane >= HD * head_row) & (head_lane < HD * head_row + HD)
    by_g = [mm(ext, g[L * a : L * a + L, :], TN) for a in range(2)]
    by_d = [mm(ext, dv[L * a : L * a + L, :], TN) for a in range(2)]
    for half in range(2):
        for r in range(5):
            i = 2 * r + half
            for m in range(2):
                for side in range(2):
                    row = 4 * r + 2 * side + m
                    out[i, m : m + 1, HALF * side : HALF * side + HALF] = sums[
                        row : row + 1, HALF * half : HALF * half + HALF
                    ]
            base = 40 * i
            val = sum(
                jnp.where(headmask, by_g[a][base + 16 * a : base + 16 * a + 16, :], 0.0)
                for a in range(2)
            )
            out[i, 2:3, :] = jnp.sum(val, axis=0, keepdims=True)
            out[i, 3:4, :] = (
                by_d[0][base + 32 : base + 33, :] + by_d[1][base + 33 : base + 34, :]
            )
    for store in stores:
        store.wait()


def final_step(got, dv, g):
    vmem = pl.BlockSpec(memory_space=pltpu.VMEM)
    hbm = pl.BlockSpec(memory_space=pl.ANY)
    return pl.pallas_call(
        final_kernel,
        out_shape=(
            jax.ShapeDtypeStruct((2, L, D), F32),
            jax.ShapeDtypeStruct((10, 4, D), F32),
        ),
        in_specs=[hbm] * 3,
        out_specs=(hbm, vmem),
        scratch_shapes=[
            pltpu.VMEM((8 * L, D), BF),
            pltpu.VMEM((2 * NDEV, D), BF),
            pltpu.VMEM((2 * NDEV, D), BF),
            pltpu.VMEM((2, L, D), F32),
            pltpu.VMEM((L, D), BF),
            pltpu.VMEM((32, D), F32),
            pltpu.SemaphoreType.DMA((6,)),
            pltpu.SemaphoreType.DMA((8,)),
        ],
        compiler_params=pltpu.CompilerParams(vmem_limit_bytes=60 * 1024 * 1024),
        cost_estimate=pl.CostEstimate(
            flops=2 * 10**9, bytes_accessed=7 * 10**6, transcendentals=0
        ),
        name="final_step",
    )(got, dv, g)


def trade(a, mask):
    return lax.ppermute(a, "dev", [(d, d ^ mask) for d in range(NDEV)])


def exchange(a, rows):
    blocks = a.reshape(NDEV, rows, a.shape[1])
    return lax.all_to_all(blocks, "dev", 0, 0, tiled=True)


def shards(embeddings, lengths, pairs, labels, w_query, w_key, w_value, w_out, w_class):
    ids = pairs.reshape(-1)
    select = (ids[:, None] == jnp.arange(2 * NDEV, dtype=jnp.int32)[None, :]).astype(BF)
    place = jnp.arange(8, dtype=jnp.int32)[None, :]
    spots = jnp.repeat(pairs, 2, axis=1)
    spots = jnp.concatenate([spots, jnp.full((NDEV, 4), -1, jnp.int32)], axis=1)
    spots = jnp.stack([jnp.where((place & 1) == n, spots, -1).reshape(-1) for n in range(2)])

    spread = lax.all_to_all(embeddings.transpose(1, 0, 2), "dev", 0, 0, tiled=True)
    picked = mm(select, spread.reshape(2 * NDEV, D)).astype(BF)
    x = exchange(picked, 2).transpose(1, 0, 2).reshape(2 * L, D)

    near, far = trade(x, 1), trade(x, 2)

    *pieces, dx, z = pair_step(
        lengths, ids, labels, x, w_class.reshape(1, D), w_query, w_key, w_value, w_out
    )
    ms = [pieces[0]] + [trade(pieces[n], n) for n in range(1, 4)]
    dx, far = lax.optimization_barrier((dx, far))
    rows = exchange(dx, 8).reshape(8 * NDEV, HALF)
    xs = [x, near, far, trade(far, 1)]
    tail = grads_step(xs, ms, z)

    last = sum_step(rows, spots, tail)
    got = exchange(last, 8).reshape(8 * NDEV, D)
    dv, g = vectors_step(rows, w_out)
    return final_step(got, dv, g)


def solution(mesh):
    placed = (P("dev", None, None), P(), P(), P("dev"), P(), P(), P(), P(), P())
    return jax.shard_map(
        shards,
        mesh=mesh,
        in_specs=placed,
        out_specs=(P("dev", None, None), P("dev", None, None)),
        check_vma=False,
    )
```

time: 213 us -> 161 us (0.76)
  blocking collectives: 52.4 us -> 0 us
  waiting for transfers between devices: 65.1 us -> 79.9 us
  Pallas kernels: 26.2 us -> 40.2 us
  local copies, waits for them, and re-layouts: 22.1 us -> 8.68 us
  starting transfers between devices: 38.2 us -> 29 us
  matrix products: 4.8 us -> 0.38 us
    all_gather x1 -> x0, blocking collectives: 52.4 us -> none  [shards(): dv_all = lax.all_gather(dv, 'dev', axis=0, tiled=True)]
    all_to_all x3, waiting for transfers between devices: 14.3 us -> 44.5 us  [exchange(): return lax.all_to_all(blocks, 'dev', 0, 0, tiled=True)]
    ppermute x11 -> x6, waiting for transfers between devices: 36.2 us -> 20.7 us  [trade(): return lax.ppermute(a, 'dev', [(d, d ^ mask) for d in range(NDEV)])]
    pallas_call x2 -> x4, Pallas kernels: 21.3 us -> 35.4 us  [the longest x1 17.6 us: pair_step(): pl.pallas_call(pair_kernel, out_shape=(jax.ShapeDtypeStruct((2 * L, HALF)...]
    reshape x5 -> x2, local copies, waits for them, and re-layouts: 10.5 us -> 1.22 us  [the longest x1 1.08 us: exchange(): blocks = a.reshape(NDEV, rows, a.shape[1])]
    ppermute x11 -> x6, starting transfers between devices: 9.87 us -> 4.17 us  [trade(): return lax.ppermute(a, 'dev', [(d, d ^ mask) for d in range(NDEV)])]
    unnamed x25 -> x18, local copies, waits for them, and re-layouts: 11.1 us -> 6.15 us
    dot_general x4 -> x1, matrix products: 4.8 us -> 0.38 us  [mm(): return lax.dot_general(a, b, dims, preferred_element_type=F32)]
  transfers between devices with their start and end apart: 15 -> 10, of which waited for: 5 -> 5; matrix products, arithmetic and copies ran while one was open for 5% -> 1% of each run, Pallas kernels for 0% -> 19%
where the time goes in v2:
time: 161 us
  waiting for transfers between devices  79.9 us (50%)
  Pallas kernels  40.2 us (25%)
  starting transfers between devices  29 us (18%)
  local copies, waits for them, and re-layouts  8.68 us (5%)
  between operations  1.66 us (1%)
    all_to_all x3, waiting for transfers between devices, exchange(): return lax.all_to_all(blocks, 'dev', 0, 0, tiled=True)  44.5 us
    ppermute x6, waiting for transfers between devices, trade(): return lax.ppermute(a, 'dev', [(d, d ^ mask) for d in range(NDEV)])  20.7 us
    pallas_call x1, Pallas kernels, pair_step(): pl.pallas_call(pair_kernel, out_shape=(jax.ShapeDtypeStruct((2 * L, HALF)...  17.6 us
    all_to_all x1, waiting for transfers between devices, shards(): lax.all_to_all(embeddings.transpose(1, 0, 2), 'dev', 0, 0, tiled=True)  14.6 us
    all_to_all x3, starting transfers between devices, exchange(): return lax.all_to_all(blocks, 'dev', 0, 0, tiled=True)  13.4 us
    all_to_all x1, starting transfers between devices, shards(): lax.all_to_all(embeddings.transpose(1, 0, 2), 'dev', 0, 0, tiled=True)  11.5 us
    pallas_call x1, Pallas kernels, grads_step(): pl.pallas_call(grads_kernel, out_shape=jax.ShapeDtypeStruct((8 * L, D), B...  7.2 us
    unnamed x18, local copies, waits for them, and re-layouts  6.15 us
  transfers between devices with their start and end apart: 10, of which 5 were waited for; matrix products, arithmetic and copies ran while one was open for 1% of the time, Pallas kernels for 19%

profile of v2, /device:TPU:1, one launch (start us, length us, event | category | flops | bytes accessed | tf_op | source)
XLA Modules:
  0.0 160.6 jit_solution(8911618241595263659)
XLA Ops:
  0.6 2.6 %copy.24 = bf16[2,128,1280]{2,0,1:T(2,128)(2,1)} copy(bf16[2,128,1280]{2,1,0:T(8,128)(2,1)} %param.9) | data formatting | bytes 1310720 | tf_op args[0]
  3.2 11.5 %all-to-all-start = ((bf16[128,2,1280]{2,1,0:T(2,128)(2,1)}), bf16[128,2,1280]{2,1,0:T(2,128)(2,1)S(1)}, u32[]{:S(2)}, u32[]{:S(2)}) async-start(bf16[128,2,1280]{2,1,0:T(2,128)(2,1)} %bitcast.10), calls=%async_computation | async-start | bytes 1310720 | tf_op jit(solution)/shard_map/all_to_all | solution.py:499
  15.0 14.6 %all-to-all-done = bf16[128,2,1280]{2,1,0:T(2,128)(2,1)S(1)} async-done(((bf16[128,2,1280]{2,1,0:T(2,128)(2,1)}), bf16[128,2,1280]{2,1,0:T(2,128)(2,1)S(1)}, u32[]{:S(2)}, u32[]{:S(2)}) %all-to-all-start) | async-done | bytes 655392 | tf_op jit(solution)/shard_map/all_to_all | solution.py:499
  30.3 1.1 reshape.47
  31.4 4.8 %all-to-all-start.1 = ((bf16[128,2,1280]{2,1,0:T(2,128)(2,1)}), bf16[128,2,1280]{2,1,0:T(2,128)(2,1)S(1)}, u32[]{:S(2)}, u32[]{:S(2)}) async-start(bf16[128,2,1280]{2,1,0:T(2,128)(2,1)} %reshape.47), calls=%async_computation.1 | async-start | bytes 1310720 | tf_op jit(solution)/shard_map/all_to_all | solution.py:488
  36.1 0.6 reshape.49.wc
  37.4 13.6 %all-to-all-done.1 = bf16[128,2,1280]{2,1,0:T(2,128)(2,1)S(1)} async-done(((bf16[128,2,1280]{2,1,0:T(2,128)(2,1)}), bf16[128,2,1280]{2,1,0:T(2,128)(2,1)S(1)}, u32[]{:S(2)}, u32[]{:S(2)}) %all-to-all-start.1) | async-done | bytes 655392 | tf_op jit(solution)/shard_map/all_to_all | solution.py:488
  51.2 1.5 collective-permute-start.1
  52.7 17.6 %pair_step.1 = (bf16[256,640]{1,0:T(8,128)(2,1)}, bf16[256,640]{1,0:T(8,128)(2,1)}, bf16[256,640]{1,0:T(8,128)(2,1)}, bf16[256,640]{1,0:T(8,128)(2,1)}, bf16[102...) custom-call(s32[256]{0:T(256)} %lengths.1, s32[256]{0:T(256)} %copy-done.5, s32[1]{0:T(128)S(6)} %copy.25.label, ...), custom_call_target="tpu_custom_call" | custom-call | flops 12000000000 | bytes 18000000 | tf_op jit(solution)/shard_map/pair_step/pallas_call | solution.py:200
  70.9 1.4 collective-permute-start.4
  72.3 0.6 collective-permute-start.5
  72.9 4.5 %all-to-all-start.2 = ((bf16[128,8,640]{2,1,0:T(8,128)(2,1)}), bf16[128,8,640]{2,1,0:T(8,128)(2,1)S(1)}, u32[]{:S(2)}, u32[]{:S(2)}) async-start(bf16[128,8,640]{2,1,0:T(8,128)(2,1)} %bitcast.14), calls=%async_computation.2 | async-start | bytes 2621440 | tf_op jit(solution)/shard_map/all_to_all | solution.py:488
  77.8 0.6 pad_add_fusion.ids
  78.4 1.7 %collective-permute-done.4.refs_6_ = bf16[256,640]{1,0:T(8,128)(2,1)} collective-permute-done((bf16[256,640]{1,0:T(8,128)(2,1)}, bf16[256,640]{1,0:T(8,128)(2,1)}, u32[]{:S(2)}, u32[]{:S(2)}) %collective-permute-start.4) | collective-permute-done | bytes 327712 | tf_op jit(solution)/shard_map/ppermute | solution.py:483
  80.2 19.0 %collective-permute-done.5.refs_7_ = bf16[256,640]{1,0:T(8,128)(2,1)} collective-permute-done((bf16[256,640]{1,0:T(8,128)(2,1)}, bf16[256,640]{1,0:T(8,128)(2,1)}, u32[]{:S(2)}, u32[]{:S(2)}) %collective-permute-start.5) | collective-permute-done | bytes 327712 | tf_op jit(solution)/shard_map/ppermute | solution.py:483
  99.2 0.9 copy-done.7
  100.0 7.2 %grads_step.1.tail_h = bf16[1024,1280]{1,0:T(8,128)(2,1)} custom-call(bf16[256,1280]{1,0:T(8,128)(2,1)} %bitcast.20, bf16[256,1280]{1,0:T(8,128)(2,1)} %copy-done.7, bf16[256,1280]{1,0:T(8,128)(2,1)} %copy-done.6, bf16[256,1280]{1,0:T(8,128)(2,1)} %collective-permute-done.2.refs_3_, bf16[256,640]{1,0:T(8,128)(2,1)} %get-tuple-element.15.refs_4_, ...), custom_call_target="tpu_custom_call" | custom-call | flops 12000000000 | bytes 7000000 | tf_op jit(solution)/shard_map/grads_step/pallas_call | solution.py:278
  107.3 1.0 copy-done.1
  108.3 5.4 %sum_step.1 = bf16[1024,1280]{1,0:T(8,128)(2,1)} custom-call(bf16[1024,640]{1,0:T(8,128)(2,1)} %bitcast.15, s32[2,1024]{1,0:T(2,128)} %pad_add_fusion.ids, bf16[1024,1280]{1,0:T(8,128)(2,1)} %grads_step.1.tail_h), custom_call_target="tpu_custom_call" | custom-call | flops 2000000000 | bytes 7000000 | tf_op jit(solution)/shard_map/sum_step/pallas_call | solution.py:340
  113.8 4.2 %all-to-all-start.3 = ((bf16[128,8,1280]{2,1,0:T(8,128)(2,1)}), bf16[128,8,1280]{2,1,0:T(8,128)(2,1)S(1)}, u32[]{:S(2)}, u32[]{:S(2)}) async-start(bf16[128,8,1280]{2,1,0:T(8,128)(2,1)} %bitcast.12), calls=%async_computation.3 | async-start | bytes 5242880 | tf_op jit(solution)/shard_map/all_to_all | solution.py:488
  118.0 5.2 %vectors_step.1 = (bf16[256,1280]{1,0:T(8,128)(2,1)}, bf16[256,1280]{1,0:T(8,128)(2,1)}) custom-call(bf16[1024,640]{1,0:T(8,128)(2,1)} %bitcast.16, bf16[1280,1280]{1,0:T(8,128)(2,1)} %wo.1), custom_call_target="tpu_custom_call" | custom-call | flops 2000000000 | bytes 6000000 | tf_op jit(solution)/shard_map/vectors_step/pallas_call | solution.py:374
  123.2 30.9 %all-to-all-done.3 = bf16[128,8,1280]{2,1,0:T(8,128)(2,1)S(1)} async-done(((bf16[128,8,1280]{2,1,0:T(8,128)(2,1)}), bf16[128,8,1280]{2,1,0:T(8,128)(2,1)S(1)}, u32[]{:S(2)}, u32[]{:S(2)}) %all-to-all-start.3) | async-done | bytes 2621472 | tf_op jit(solution)/shard_map/all_to_all | solution.py:488
  154.0 1.5 copy-done
  155.5 4.8 %final_step.1 = (f32[2,128,1280]{2,1,0:T(8,128)}, f32[10,4,1280]{2,1,0:T(4,128)}) custom-call(bf16[1024,1280]{1,0:T(8,128)(2,1)} %bitcast.11, bf16[256,1280]{1,0:T(8,128)(2,1)} %get-tuple-element.20.dv_h, bf16[256,1280]{1,0:T(8,128)(2,1)} %get-tuple-element.21.g_h), custom_call_target="tpu_custom_call" | custom-call | flops 2000000000 | bytes 7000000 | tf_op jit(solution)/shard_map/final_step/pallas_call | solution.py:456
  (33 shorter events, 2.2 us)
Async XLA Ops:
  0.6 14.1 %copy-start.4 = (s32[128,2]{0,1:T(2,128)S(1)}, s32[128,2]{0,1:T(2,128)}, u32[]{:S(2)}) copy-start(s32[128,2]{0,1:T(2,128)} %param.11) | copy-start | bytes 3076
  3.2 26.4 %all-to-all-start = ((bf16[128,2,1280]{2,1,0:T(2,128)(2,1)}), bf16[128,2,1280]{2,1,0:T(2,128)(2,1)S(1)}, u32[]{:S(2)}, u32[]{:S(2)}) async-start(bf16[128,2,1280]{2,1,0:T(2,128)(2,1)} %bitcast.10), calls=%async_computation | async-start | bytes 1310720 | tf_op jit(solution)/shard_map/all_to_all | solution.py:499
  15.0 16.4 %copy-start.5 = (s32[256]{0:T(256)}, s32[256]{0:T(256)S(1)}, u32[]{:S(2)}) copy-start(s32[256]{0:T(256)S(1)} %reshape.45.pairs) | copy-start | bytes 3076
  15.0 21.1 %copy-start.3 = (f32[1280]{0:T(1024)S(1)}, f32[1280]{0:T(1024)}, u32[]{:S(2)}) copy-start(f32[1280]{0:T(1024)} %param.17) | copy-start | bytes 15364
  31.4 19.7 %all-to-all-start.1 = ((bf16[128,2,1280]{2,1,0:T(2,128)(2,1)}), bf16[128,2,1280]{2,1,0:T(2,128)(2,1)S(1)}, u32[]{:S(2)}, u32[]{:S(2)}) async-start(bf16[128,2,1280]{2,1,0:T(2,128)(2,1)} %reshape.47), calls=%async_computation.1 | async-start | bytes 1310720 | tf_op jit(solution)/shard_map/all_to_all | solution.py:488
  51.1 1.6 %copy-start.2 = (bf16[2,128,1280]{2,1,0:T(8,128)(2,1)}, bf16[2,128,1280]{2,1,0:T(8,128)(2,1)S(1)}, u32[]{:S(2)}) copy-start(bf16[2,128,1280]{2,1,0:T(8,128)(2,1)S(1)} %copy.20) | copy-start | bytes 1966084
  51.1 19.2 %collective-permute-start = (bf16[256,1280]{1,0:T(8,128)(2,1)S(1)}, bf16[256,1280]{1,0:T(8,128)(2,1)S(1)}, u32[]{:S(2)}, u32[]{:S(2)}) collective-permute-start(bf16[256,1280]{1,0:T(8,128)(2,1)S(1)} %bitcast.17), channel_id=1, source_target_pairs={{0,2},{1,3},{2,0},{3,1},{4,6},{5,7},{6,4},{7,5},{8,10},{9,11},{10,... | collective-permute-start | bytes 1966088 | tf_op jit(solution)/shard_map/ppermute | solution.py:483
  51.2 48.0 %collective-permute-start.1 = (bf16[256,1280]{1,0:T(8,128)(2,1)S(1)}, bf16[256,1280]{1,0:T(8,128)(2,1)S(1)}, u32[]{:S(2)}, u32[]{:S(2)}) collective-permute-start(bf16[256,1280]{1,0:T(8,128)(2,1)S(1)} %bitcast.18), channel_id=1, source_target_pairs={{0,1},{1,0},{2,3},{3,2},{4,5},{5,4},{6,7},{7,6},{8,9},{9,8},{10,11... | collective-permute-start | bytes 1966088 | tf_op jit(solution)/shard_map/ppermute | solution.py:483
  70.3 28.9 %copy-start.6 = (bf16[256,1280]{1,0:T(8,128)(2,1)}, bf16[256,1280]{1,0:T(8,128)(2,1)S(1)}, u32[]{:S(2)}) copy-start(bf16[256,1280]{1,0:T(8,128)(2,1)S(1)} %collective-permute-done.refs_2_) | copy-start | bytes 1966084
  70.3 28.9 %collective-permute-start.2 = (bf16[256,1280]{1,0:T(8,128)(2,1)S(1)}, bf16[256,1280]{1,0:T(8,128)(2,1)}, u32[]{:S(2)}, u32[]{:S(2)}) collective-permute-start(bf16[256,1280]{1,0:T(8,128)(2,1)S(1)} %collective-permute-done.refs_2_), channel_id=1, source_target_pairs={{0,1},{1,0},{2,3},{3,2},{4,5},{5,4},{6,7},{7,6},{8,9},{9,8},{10,11... | collective-permute-start | bytes 1966088 | tf_op jit(solution)/shard_map/ppermute | solution.py:483
  70.7 7.7 %collective-permute-start.3 = (bf16[256,640]{1,0:T(8,128)(2,1)}, bf16[256,640]{1,0:T(8,128)(2,1)}, u32[]{:S(2)}, u32[]{:S(2)}) collective-permute-start(bf16[256,640]{1,0:T(8,128)(2,1)} %get-tuple-element.16), channel_id=1, source_target_pairs={{0,1},{1,0},{2,3},{3,2},{4,5},{5,4},{6,7},{7,6},{8,9},{9,8},{10,11... | collective-permute-start | bytes 983048 | tf_op jit(solution)/shard_map/ppermute | solution.py:483
  70.9 9.3 %collective-permute-start.4 = (bf16[256,640]{1,0:T(8,128)(2,1)}, bf16[256,640]{1,0:T(8,128)(2,1)}, u32[]{:S(2)}, u32[]{:S(2)}) collective-permute-start(bf16[256,640]{1,0:T(8,128)(2,1)} %get-tuple-element.17), channel_id=1, source_target_pairs={{0,2},{1,3},{2,0},{3,1},{4,6},{5,7},{6,4},{7,5},{8,10},{9,11},{10,... | collective-permute-start | bytes 983048 | tf_op jit(solution)/shard_map/ppermute | solution.py:483
  72.3 26.9 %collective-permute-start.5 = (bf16[256,640]{1,0:T(8,128)(2,1)}, bf16[256,640]{1,0:T(8,128)(2,1)}, u32[]{:S(2)}, u32[]{:S(2)}) collective-permute-start(bf16[256,640]{1,0:T(8,128)(2,1)} %get-tuple-element.18), channel_id=1, source_target_pairs={{0,3},{1,2},{2,1},{3,0},{4,7},{5,6},{6,5},{7,4},{8,11},{9,10},{10,... | collective-permute-start | bytes 983048 | tf_op jit(solution)/shard_map/ppermute | solution.py:483
  72.9 34.4 %all-to-all-start.2 = ((bf16[128,8,640]{2,1,0:T(8,128)(2,1)}), bf16[128,8,640]{2,1,0:T(8,128)(2,1)S(1)}, u32[]{:S(2)}, u32[]{:S(2)}) async-start(bf16[128,8,640]{2,1,0:T(8,128)(2,1)} %bitcast.14), calls=%async_computation.2 | async-start | bytes 2621440 | tf_op jit(solution)/shard_map/all_to_all | solution.py:488
  99.2 0.9 copy-start.7
  107.3 1.1 copy-start.1
  113.8 40.3 %all-to-all-start.3 = ((bf16[128,8,1280]{2,1,0:T(8,128)(2,1)}), bf16[128,8,1280]{2,1,0:T(8,128)(2,1)S(1)}, u32[]{:S(2)}, u32[]{:S(2)}) async-start(bf16[128,8,1280]{2,1,0:T(8,128)(2,1)} %bitcast.12), calls=%async_computation.3 | async-start | bytes 5242880 | tf_op jit(solution)/shard_map/all_to_all | solution.py:488
  154.0 1.5 copy-start

commit v3 on v2

--- a/solution.py
+++ b/solution.py
@@ -13,6 +13,7 @@
 D = 1280
 NDEV = 128
 HALF = 640
+WIDE = 512
 BF = jnp.bfloat16
 F32 = jnp.float32
 NN = (((1,), (0,)), ((), ()))
@@ -40,22 +41,40 @@
     pieces_h, (dx_h, z) = refs[:4], refs[4:6]
     x, wq, wk, wv, wo, q, k, p, s, u, dqk, dqb, dkb, back, woven, pieces, dx, sems, out_sems = refs[6:]
     dev = lax.axis_index("dev")
-    loads = []
-    for n, (src, dst) in enumerate(((x_h, x), (wq_h, wq), (wk_h, wk), (wv_h, wv), (wo_h, wo))):
-        load = pltpu.make_async_copy(src, dst, sems.at[n])
-        load.start()
-        loads.append(load)
+    top, low_half = (slice(0, D // 2), slice(None)), (slice(D // 2, D), slice(None))
+    loads = [[pltpu.make_async_copy(x_h, x, sems.at[0])]]
+    for n, (src, dst) in enumerate(((wq_h, wq), (wk_h, wk), (wv_h, wv), (wo_h, wo))):
+        loads.append(
+            [
+                pltpu.make_async_copy(src.at[half], dst.at[half], sems.at[2 * n + 1 + m])
+                for m, half in enumerate((top, low_half))
+            ]
+        )
+
+    def fetch(n):
+        for load in loads[n]:
+            load.start()
+
+    def arrive(n):
+        for load in loads[n]:
+            load.wait()
+
+    fetch(0)
+    fetch(1)
     lens = [lengths[pairs[2 * dev]], lengths[pairs[2 * dev + 1]]]
     rows = iota((L, L), 0)
     lanes = iota((L, L), 1)
     scale = HD ** (-0.5)
 
-    loads[0].wait()
-    loads[1].wait()
+    arrive(0)
+    arrive(1)
+    fetch(2)
     for n in range(5):
         cols = slice(256 * n, 256 * n + 256)
         q[:, cols] = mm(x[...], wq[:, cols]).astype(BF)
-    loads[2].wait()
+    arrive(2)
+    fetch(3)
+    fetch(4)
     for n in range(5):
         cols = slice(256 * n, 256 * n + 256)
         k[:, cols] = mm(x[...], wk[:, cols]).astype(BF)
@@ -92,9 +111,9 @@
         hi, lo = split(s[a * HEADS : a * HEADS + HEADS, :])
         ys.append(mm(hi, x[L * b : L * b + L, :]) + mm(lo, x[L * b : L * b + L, :]))
     y = jnp.concatenate(ys, axis=0)
-    y_hi, y_lo = split(y)
-    loads[3].wait()
-    t = mm(y_hi, wv[...]) + mm(y_lo, wv[...])
+    arrive(3)
+    t = mm(jnp.concatenate(split(y), axis=0), wv[...])
+    t = t[0 : 2 * HEADS, :] + t[2 * HEADS :, :]
     pooled_ctx = [
         jnp.sum(jnp.where(headmask, t[HEADS * a : HEADS * a + HEADS, :], 0.0), axis=0, keepdims=True)
         for a in range(2)
@@ -108,9 +127,9 @@
         (mask_row == 1) & (mask_lane >= L) & (mask_lane < L + lens[1])
     )
     x_sum = mm(jnp.where(mask8, 1.0, 0.0).astype(BF), x[...])
-    ctx_hi, ctx_lo = split(ctx8)
-    loads[4].wait()
-    total = x_sum + mm(ctx_hi, wo[...]) + mm(ctx_lo, wo[...])
+    arrive(4)
+    mixed = mm(jnp.concatenate(split(ctx8), axis=0), wo[...])
+    total = x_sum + mixed[0:8, :] + mixed[8:16, :]
     lens_f = [n.astype(F32) for n in lens]
     pooled = [total[0:1, :] / lens_f[0], total[1:2, :] / lens_f[1]]
     logit = jnp.sum(wc[...] * pooled[0] * pooled[1], axis=1, keepdims=True)
@@ -173,18 +192,21 @@
             val = acc[L * c : L * c + L, :] + mm(s_b[part, :], gv_hi[part, cols], TN)
             val = val + jnp.where(tall < lens[c], dvec[c][:, cols], 0.0)
             back[L * c : L * c + L, cols] = val
+    odd = (iota((L, D), 0) & 1) == 1
+    shared = jnp.where(odd, dvec[1], dvec[0])
     for c in range(2):
-        for half in range(2):
-            row = 2 * c + half
-            for n in range(5):
-                cols = slice(HALF * half + L * n, HALF * half + L * n + L)
-                woven[n, pl.ds(row, L, stride=8), :] = back[L * c : L * c + L, cols]
-                woven[n, pl.ds(row + 4, L, stride=8), :] = jnp.broadcast_to(
-                    dvec[c][:, cols], (L, L)
-                )
+        for n in range(10):
+            woven[n % 4, pl.ds(3 * c + n // 4, L, stride=8), :] = back[
+                L * c : L * c + L, L * n : L * n + L
+            ]
+    for n in range(8):
+        woven[n % 4, pl.ds(6 + n // 4, L, stride=8), :] = shared[:, L * n : L * n + L]
+    for n in range(2):
+        woven[2 + n, pl.ds(2, L, stride=8), :] = shared[:, L * (8 + n) : L * (9 + n)]
+        woven[2 + n, pl.ds(5, L, stride=8), :] = jnp.zeros((L, L), F32)
     for n in range(4):
         part = slice(256 * n, 256 * n + 256)
-        for m in range(5):
+        for m in range(4):
             dx[part, L * m : L * m + L] = woven[m, part, :].astype(BF)
         store = pltpu.make_async_copy(dx.at[part, :], dx_h.at[part, :], out_sems.at[4 + n])
         store.start()
@@ -201,7 +223,7 @@
         pair_kernel,
         out_shape=(jax.ShapeDtypeStruct((2 * L, HALF), BF),) * 4
         + (
-            jax.ShapeDtypeStruct((8 * L, HALF), BF),
+            jax.ShapeDtypeStruct((8 * L, WIDE), BF),
             jax.ShapeDtypeStruct((40, D), BF),
         ),
         in_specs=[smem, smem, smem, hbm, vmem, hbm, hbm, hbm, hbm],
@@ -218,10 +240,10 @@
             pltpu.VMEM((2 * L, D), BF),
             pltpu.VMEM((2 * L, D), BF),
             pltpu.VMEM((2 * L, D), F32),
-            pltpu.VMEM((5, 8 * L, L), F32),
+            pltpu.VMEM((4, 8 * L, L), F32),
             pltpu.VMEM((4, 2 * L, HALF), BF),
-            pltpu.VMEM((8 * L, HALF), BF),
-            pltpu.SemaphoreType.DMA((5,)),
+            pltpu.VMEM((8 * L, WIDE), BF),
+            pltpu.SemaphoreType.DMA((9,)),
             pltpu.SemaphoreType.DMA((8,)),
         ],
         compiler_params=pltpu.CompilerParams(vmem_limit_bytes=60 * 1024 * 1024),
@@ -232,18 +254,39 @@
     )(lengths, pairs, label, x, wc, wq, wk, wv, wo)
 
 
-def grads_kernel(*refs):
-    ins, z, out_h = refs[:8], refs[8], refs[9]
-    xs, ms, sums, zt, woven, out, sems, out_sems = refs[10:]
+def turn_kernel(z, *refs):
+    unit = jnp.where(iota((40, L), 0) == iota((40, L), 1), 1.0, 0.0).astype(BF)
+    refs[-1][...] = mm(z[...], unit, TN)
+
+
+def turn_step(z, ms):
+    vmem = pl.BlockSpec(memory_space=pltpu.VMEM)
+    hbm = pl.BlockSpec(memory_space=pl.ANY)
+    return pl.pallas_call(
+        turn_kernel,
+        out_shape=jax.ShapeDtypeStruct((D, L), F32),
+        in_specs=[vmem] + [hbm] * 3,
+        out_specs=vmem,
+        compiler_params=pltpu.CompilerParams(vmem_limit_bytes=60 * 1024 * 1024),
+        cost_estimate=pl.CostEstimate(
+            flops=12 * 10**9, bytes_accessed=7 * 10**6, transcendentals=0
+        ),
+        name="turn_step",
+    )(z, *ms)
+
+
+def merge_kernel(*refs):
+    ins, zt_h, rows_h, ids, out_h = refs[:8], refs[8], refs[9], refs[10], refs[11]
+    xs, ms, zt, rows, sums, woven, out, sems, out_sems = refs[12:]
     loads = []
     for n in range(4):
         loads.append(pltpu.make_async_copy(ins[n], xs.at[n], sems.at[n]))
         loads.append(pltpu.make_async_copy(ins[4 + n], ms.at[n], sems.at[4 + n]))
+    loads.append(pltpu.make_async_copy(rows_h, rows, sems.at[8]))
+    loads.append(pltpu.make_async_copy(zt_h, zt, sems.at[9]))
     for load in loads:
         load.start()
-    unit = jnp.where(iota((40, L), 0) == iota((40, L), 1), 1.0, 0.0).astype(BF)
-    zt[...] = mm(z[...], unit, TN)
-    for load in loads:
+    for load in loads[:8]:
         load.wait()
     for n in range(5):
         cols = slice(256 * n, 256 * n + 256)
@@ -251,12 +294,23 @@
         for m in range(4):
             term = mm(xs[m, :, cols], ms[m], TN)
             acc = term if acc is None else acc + term
-        for half in range(5):
-            sums[half, cols, :] = acc[:, L * half : L * half + L]
+        for m in range(5):
+            sums[m, cols, :] = acc[:, L * m : L * m + L]
+    loads[8].wait()
+    loads[9].wait()
+    row = iota((2 * NDEV, 8 * L), 0)
+    chain = 2 * (row & 127) + (row >> 7)
+    for n in range(3):
+        tiles = 4 if n < 2 else 2
+        select = jnp.where(chain == ids[n : n + 1, :], 1.0, 0.0).astype(BF)
+        summed = mm(select, rows[:, 0 : L * tiles])
+        for c in range(2):
+            for m in range(tiles):
+                woven[4 * n + m, pl.ds(c, L, stride=8), :] = summed[
+                    L * c : L * c + L, L * m : L * m + L
+                ]
     for i in range(10):
         pick = pl.ds(i, L, stride=10)
-        for row in range(2):
-            woven[i, pl.ds(row, L, stride=8), :] = jnp.zeros((L, L), F32)
         for n in range(5):
             woven[5 * (i % 2) + n, pl.ds(2 + i // 2, L, stride=8), :] = sums[n, pick, :]
         woven[i, pl.ds(7, L, stride=8), :] = zt[pick, :]
@@ -272,127 +326,82 @@
         store.wait()
 
 
-def grads_step(xs, ms, z):
+def merge_step(xs, ms, zt, rows, ids):
     vmem = pl.BlockSpec(memory_space=pltpu.VMEM)
     hbm = pl.BlockSpec(memory_space=pl.ANY)
     return pl.pallas_call(
-        grads_kernel,
+        merge_kernel,
         out_shape=jax.ShapeDtypeStruct((8 * L, D), BF),
-        in_specs=[hbm] * 8 + [vmem],
+        in_specs=[hbm] * 10 + [vmem],
         out_specs=hbm,
         scratch_shapes=[
             pltpu.VMEM((4, 2 * L, D), BF),
             pltpu.VMEM((4, 2 * L, HALF), BF),
+            pltpu.VMEM((D, L), F32),
+            pltpu.VMEM((8 * L, WIDE), BF),
             pltpu.VMEM((5, D, L), F32),
-            pltpu.VMEM((D, L), F32),
             pltpu.VMEM((10, 8 * L, L), F32),
             pltpu.VMEM((8 * L, D), BF),
-            pltpu.SemaphoreType.DMA((8,)),
+            pltpu.SemaphoreType.DMA((10,)),
             pltpu.SemaphoreType.DMA((4,)),
         ],
         compiler_params=pltpu.CompilerParams(vmem_limit_bytes=60 * 1024 * 1024),
         cost_estimate=pl.CostEstimate(
-            flops=12 * 10**9, bytes_accessed=7 * 10**6, transcendentals=0
-        ),
-        name="grads_step",
-    )(*xs, *ms, z)
-
-
-def sum_kernel(rows_h, ids, tail_h, out_h, rows, tail, out, sems, out_sems):
-    loads = []
-    for n in range(4):
-        part = (slice(256 * n, 256 * n + 256), slice(None))
-        loads.append(pltpu.make_async_copy(rows_h.at[part], rows.at[part], sems.at[n]))
-    for n in range(4):
-        part = (slice(256 * n, 256 * n + 256), slice(None))
-        loads.append(pltpu.make_async_copy(tail_h.at[part], tail.at[part], sems.at[4 + n]))
-    for load in loads:
-        load.start()
-    chain = iota((2 * NDEV, 256), 0)
-    halves = [None, None]
-    for n in range(4):
-        part = slice(256 * n, 256 * n + 256)
-        loads[n].wait()
-        for half in range(2):
-            select = jnp.where(chain == ids[half : half + 1, part], 1.0, 0.0).astype(BF)
-            term = mm(select, rows[part, :])
-            halves[half] = term if n == 0 else halves[half] + term
-    summed = jnp.concatenate(halves, axis=1).astype(BF)
-    stores = []
-    for n in range(4):
-        part = slice(256 * n, 256 * n + 256)
-        to = iota((256, 64), 0)
-        frm = iota((256, 64), 1)
-        weave = jnp.where(to == 8 * (frm >> 1) + (frm & 1), 1.0, 0.0).astype(BF)
-        val = mm(weave, summed[64 * n : 64 * n + 64, :])
-        loads[4 + n].wait()
-        out[part, :] = (val + tail[part, :].astype(F32)).astype(BF)
-        store = pltpu.make_async_copy(out.at[part, :], out_h.at[part, :], out_sems.at[n])
-        store.start()
-        stores.append(store)
-    for store in stores:
-        store.wait()
-
-
-def sum_step(rows, ids, tail):
+            flops=4 * 10**9, bytes_accessed=7 * 10**6, transcendentals=0
+        ),
+        name="merge_step",
+    )(*xs, *ms, zt, rows, ids)
+
+
+def half_kernel(rows, out):
+    to = iota((L, 8 * L), 0)
+    frm = iota((L, 8 * L), 1)
+    picks = [jnp.where(frm == 8 * to + n, 1.0, 0.0).astype(BF) for n in (6, 7, 2)]
+    out[:, 0:512] = mm(picks[0], rows[...]).astype(BF)
+    out[:, 512:1024] = mm(picks[1], rows[...]).astype(BF)
+    out[:, 1024:D] = mm(picks[2], rows[:, 256:512]).astype(BF)
+
+
+def half_step(rows):
     vmem = pl.BlockSpec(memory_space=pltpu.VMEM)
-    hbm = pl.BlockSpec(memory_space=pl.ANY)
     return pl.pallas_call(
-        sum_kernel,
-        out_shape=jax.ShapeDtypeStruct((8 * L, D), BF),
-        in_specs=[hbm, vmem, hbm],
-        out_specs=hbm,
-        scratch_shapes=[
-            pltpu.VMEM((8 * L, HALF), BF),
-            pltpu.VMEM((8 * L, D), BF),
-            pltpu.VMEM((8 * L, D), BF),
-            pltpu.SemaphoreType.DMA((8,)),
-            pltpu.SemaphoreType.DMA((4,)),
-        ],
+        half_kernel,
+        out_shape=jax.ShapeDtypeStruct((L, D), BF),
+        in_specs=[vmem],
+        out_specs=vmem,
         compiler_params=pltpu.CompilerParams(vmem_limit_bytes=60 * 1024 * 1024),
         cost_estimate=pl.CostEstimate(
-            flops=2 * 10**9, bytes_accessed=7 * 10**6, transcendentals=0
-        ),
-        name="sum_step",
-    )(rows, ids, tail)
-
-
-def vectors_kernel(rows, wo, dv, g):
-    to = iota((2 * NDEV, 8 * L), 0)
-    frm = iota((2 * NDEV, 8 * L), 1)
-    for n in range(2):
-        place = frm == 8 * (to & 127) + 4 + 2 * (to >> 7) + n
-        pick = jnp.where(place, 1.0, 0.0).astype(BF)
-        dv[:, HALF * n : HALF * n + HALF] = mm(pick, rows[...]).astype(BF)
+            flops=10**8, bytes_accessed=10**6, transcendentals=0
+        ),
+        name="half_step",
+    )(rows)
+
+
+def vectors_kernel(own, other, wo, dv, g):
+    core = lax.axis_index("dev") & 1
+    dv[pl.ds(pl.multiple_of(core * L, L), L), :] = own[...]
+    dv[pl.ds(pl.multiple_of((1 - core) * L, L), L), :] = other[...]
     for n in range(5):
         cols = slice(256 * n, 256 * n + 256)
         g[:, cols] = mm(dv[...], wo[cols, :], NT).astype(BF)
 
 
-def vectors_step(rows, wo):
+def vectors_step(own, other, wo):
     vmem = pl.BlockSpec(memory_space=pltpu.VMEM)
     return pl.pallas_call(
         vectors_kernel,
         out_shape=(jax.ShapeDtypeStruct((2 * NDEV, D), BF),) * 2,
-        in_specs=[vmem] * 2,
+        in_specs=[vmem] * 3,
         out_specs=(vmem,) * 2,
         compiler_params=pltpu.CompilerParams(vmem_limit_bytes=60 * 1024 * 1024),
         cost_estimate=pl.CostEstimate(
             flops=2 * 10**9, bytes_accessed=6 * 10**6, transcendentals=0
         ),
         name="vectors_step",
-    )(rows, wo)
-
-
-def final_kernel(got_h, dv_h, g_h, emb_h, out, got, dv, g, emb, wide, sums, sems, out_sems):
-    loads = []
-    for n in range(4):
-        part = (slice(256 * n, 256 * n + 256), slice(None))
-        loads.append(pltpu.make_async_copy(got_h.at[part], got.at[part], sems.at[n]))
-    loads.append(pltpu.make_async_copy(dv_h, dv, sems.at[4]))
-    loads.append(pltpu.make_async_copy(g_h, g, sems.at[5]))
-    for load in loads:
-        load.start()
+    )(own, other, wo)
+
+
+def final_kernel(got, dv, g, emb_h, out, emb, wide, sums, out_sems):
     kind = iota((L, 256), 0)
     src = iota((L, 256), 1)
     t = src & 7
@@ -403,7 +412,6 @@
     pick = jnp.where(want, 1.0, 0.0).astype(BF)
     stores = []
     for n in range(4):
-        loads[n].wait()
         val = mm(pick, got[256 * n : 256 * n + 256, :])
         part = slice(32 * n, 32 * n + 32)
         for c in range(2):
@@ -421,8 +429,6 @@
         term = mm(wide[:, L * i : L * i + L], jnp.where(place, 1.0, 0.0).astype(BF))
         ext = term if ext is None else ext + term
     ext = ext.astype(BF)
-    loads[4].wait()
-    loads[5].wait()
     head_lane = iota((HEADS, D), 1)
     head_row = iota((HEADS, D), 0)
     headmask = (head_lane >= HD * head_row) & (head_lane < HD * head_row + HD)
@@ -459,19 +465,15 @@
             jax.ShapeDtypeStruct((2, L, D), F32),
             jax.ShapeDtypeStruct((10, 4, D), F32),
         ),
-        in_specs=[hbm] * 3,
+        in_specs=[vmem] * 3,
         out_specs=(hbm, vmem),
         scratch_shapes=[
-            pltpu.VMEM((8 * L, D), BF),
-            pltpu.VMEM((2 * NDEV, D), BF),
-            pltpu.VMEM((2 * NDEV, D), BF),
             pltpu.VMEM((2, L, D), F32),
             pltpu.VMEM((L, D), BF),
             pltpu.VMEM((32, D), F32),
-            pltpu.SemaphoreType.DMA((6,)),
             pltpu.SemaphoreType.DMA((8,)),
         ],
-        compiler_params=pltpu.CompilerParams(vmem_limit_bytes=60 * 1024 * 1024),
+        compiler_params=pltpu.CompilerParams(vmem_limit_bytes=24 * 1024 * 1024),
         cost_estimate=pl.CostEstimate(
             flops=2 * 10**9, bytes_accessed=7 * 10**6, transcendentals=0
         ),
@@ -492,9 +494,9 @@
     ids = pairs.reshape(-1)
     select = (ids[:, None] == jnp.arange(2 * NDEV, dtype=jnp.int32)[None, :]).astype(BF)
     place = jnp.arange(8, dtype=jnp.int32)[None, :]
-    spots = jnp.repeat(pairs, 2, axis=1)
-    spots = jnp.concatenate([spots, jnp.full((NDEV, 4), -1, jnp.int32)], axis=1)
-    spots = jnp.stack([jnp.where((place & 1) == n, spots, -1).reshape(-1) for n in range(2)])
+    spots = jnp.concatenate([jnp.repeat(pairs, 3, axis=1), jnp.full((NDEV, 2), -1, jnp.int32)], axis=1)
+    part = jnp.where(place < 6, place % 3, -1)
+    spots = jnp.stack([jnp.where(part == n, spots, -1).reshape(-1) for n in range(3)])
 
     spread = lax.all_to_all(embeddings.transpose(1, 0, 2), "dev", 0, 0, tiled=True)
     picked = mm(select, spread.reshape(2 * NDEV, D)).astype(BF)
@@ -507,13 +509,13 @@
     )
     ms = [pieces[0]] + [trade(pieces[n], n) for n in range(1, 4)]
     dx, far = lax.optimization_barrier((dx, far))
-    rows = exchange(dx, 8).reshape(8 * NDEV, HALF)
+    rows = exchange(dx, 8).reshape(8 * NDEV, WIDE)
     xs = [x, near, far, trade(far, 1)]
-    tail = grads_step(xs, ms, z)
-
-    last = sum_step(rows, spots, tail)
+    zt = turn_step(z, ms[1:])
+    last = merge_step(xs, ms, zt, rows, spots)
     got = exchange(last, 8).reshape(8 * NDEV, D)
-    dv, g = vectors_step(rows, w_out)
+    own = half_step(rows)
+    dv, g = vectors_step(own, trade(own, 1), w_out)
     return final_step(got, dv, g)
 
 

time: 161 us -> 157 us (0.975)
  waiting for transfers between devices: 79.9 us -> 73.1 us
  Pallas kernels: 40.2 us -> 37.1 us
  starting transfers between devices: 29 us -> 32.1 us
  local copies, waits for them, and re-layouts: 8.68 us -> 10.9 us
    all_to_all x3, waiting for transfers between devices: 44.5 us -> 39.9 us  [exchange(): return lax.all_to_all(blocks, 'dev', 0, 0, tiled=True)]
    all_to_all x3, starting transfers between devices: 13.4 us -> 15.8 us  [exchange(): return lax.all_to_all(blocks, 'dev', 0, 0, tiled=True)]
    unnamed x18 -> x24, local copies, waits for them, and re-layouts: 6.15 us -> 8.19 us
    pallas_call x1, Pallas kernels: 4.84 us -> 3.18 us  [final_step(): pl.pallas_call(final_kernel, out_shape=(jax.ShapeDtypeStruct((2, L, D), F...]
    ppermute x6 -> x7, waiting for transfers between devices: 20.7 us -> 19.3 us  [trade(): return lax.ppermute(a, 'dev', [(d, d ^ mask) for d in range(NDEV)])]
    ppermute x6 -> x7, starting transfers between devices: 4.17 us -> 4.78 us  [trade(): return lax.ppermute(a, 'dev', [(d, d ^ mask) for d in range(NDEV)])]
    pallas_call x2 -> x3, Pallas kernels: 12.6 us -> 13.1 us  [the longest x1 8.6 us: merge_step(): pl.pallas_call(merge_kernel, out_shape=jax.ShapeDtypeStruct((8 * L, D), B...]
  transfers between devices with their start and end apart: 10 -> 11, of which waited for: 5 -> 6; matrix products, arithmetic and copies ran while one was open for 1% -> 2% of each run, Pallas kernels for 19% -> 16%
where the time goes in v3:
time: 157 us; the launch traced here: 156 us
  waiting for transfers between devices  73.1 us (47%)
  Pallas kernels  37.1 us (24%)
  starting transfers between devices  32.1 us (20%)
  local copies, waits for them, and re-layouts  10.9 us (7%)
  between operations  1.66 us (1%)
    all_to_all x3, waiting for transfers between devices, exchange(): return lax.all_to_all(blocks, 'dev', 0, 0, tiled=True)  39.9 us
    ppermute x7, waiting for transfers between devices, trade(): return lax.ppermute(a, 'dev', [(d, d ^ mask) for d in range(NDEV)])  19.3 us
    pallas_call x1, Pallas kernels, pair_step(): pl.pallas_call(pair_kernel, out_shape=(jax.ShapeDtypeStruct((2 * L, HALF)...  16.8 us
    all_to_all x3, starting transfers between devices, exchange(): return lax.all_to_all(blocks, 'dev', 0, 0, tiled=True)  15.8 us
    all_to_all x1, waiting for transfers between devices, shards(): lax.all_to_all(embeddings.transpose(1, 0, 2), 'dev', 0, 0, tiled=True)  14 us
    all_to_all x1, starting transfers between devices, shards(): lax.all_to_all(embeddings.transpose(1, 0, 2), 'dev', 0, 0, tiled=True)  11.5 us
    pallas_call x1, Pallas kernels, merge_step(): pl.pallas_call(merge_kernel, out_shape=jax.ShapeDtypeStruct((8 * L, D), B...  8.6 us
    unnamed x24, local copies, waits for them, and re-layouts  8.19 us
  transfers between devices with their start and end apart: 11, of which 6 were waited for; matrix products, arithmetic and copies ran while one was open for 2% of the time, Pallas kernels for 16%

profile of v3, /device:TPU:1, one launch (start us, length us, event | category | flops | bytes accessed | tf_op | source)
XLA Modules:
  0.0 156.0 jit_solution(5567967082219281428)
XLA Ops:
  0.6 2.6 %copy.26 = bf16[2,128,1280]{2,0,1:T(2,128)(2,1)} copy(bf16[2,128,1280]{2,1,0:T(8,128)(2,1)} %param.9) | data formatting | bytes 1310720 | tf_op args[0]
  3.2 11.5 %all-to-all-start = ((bf16[128,2,1280]{2,1,0:T(2,128)(2,1)}), bf16[128,2,1280]{2,1,0:T(2,128)(2,1)S(1)}, u32[]{:S(2)}, u32[]{:S(2)}) async-start(bf16[128,2,1280]{2,1,0:T(2,128)(2,1)} %bitcast.11), calls=%async_computation | async-start | bytes 1310720 | tf_op jit(solution)/shard_map/all_to_all | solution.py:501
  15.7 14.0 %all-to-all-done = bf16[128,2,1280]{2,1,0:T(2,128)(2,1)S(1)} async-done(((bf16[128,2,1280]{2,1,0:T(2,128)(2,1)}), bf16[128,2,1280]{2,1,0:T(2,128)(2,1)S(1)}, u32[]{:S(2)}, u32[]{:S(2)}) %all-to-all-start) | async-done | bytes 655392 | tf_op jit(solution)/shard_map/all_to_all | solution.py:501
  30.3 1.1 reshape.63
  31.4 4.8 %all-to-all-start.1 = ((bf16[128,2,1280]{2,1,0:T(2,128)(2,1)}), bf16[128,2,1280]{2,1,0:T(2,128)(2,1)S(1)}, u32[]{:S(2)}, u32[]{:S(2)}) async-start(bf16[128,2,1280]{2,1,0:T(2,128)(2,1)} %reshape.63), calls=%async_computation.1 | async-start | bytes 1310720 | tf_op jit(solution)/shard_map/all_to_all | solution.py:490
  37.4 13.6 %all-to-all-done.1 = bf16[128,2,1280]{2,1,0:T(2,128)(2,1)S(1)} async-done(((bf16[128,2,1280]{2,1,0:T(2,128)(2,1)}), bf16[128,2,1280]{2,1,0:T(2,128)(2,1)S(1)}, u32[]{:S(2)}, u32[]{:S(2)}) %all-to-all-start.1) | async-done | bytes 655392 | tf_op jit(solution)/shard_map/all_to_all | solution.py:490
  51.9 16.8 %pair_step.1 = (bf16[256,640]{1,0:T(8,128)(2,1)}, bf16[256,640]{1,0:T(8,128)(2,1)}, bf16[256,640]{1,0:T(8,128)(2,1)}, bf16[256,640]{1,0:T(8,128)(2,1)}, bf16[102...) custom-call(s32[256]{0:T(256)} %lengths.1, s32[256]{0:T(256)} %copy-done.6, s32[1]{0:T(128)S(6)} %copy.27.label, ...), custom_call_target="tpu_custom_call" | custom-call | flops 12000000000 | bytes 18000000 | tf_op jit(solution)/shard_map/pair_step/pallas_call | solution.py:222
  68.7 1.2 collective-permute-start.3
  69.9 1.2 collective-permute-start.4
  73.5 4.5 %all-to-all-start.2 = ((bf16[128,8,512]{2,1,0:T(8,128)(2,1)}), bf16[128,8,512]{2,1,0:T(8,128)(2,1)S(1)}, u32[]{:S(2)}, u32[]{:S(2)}) async-start(bf16[128,8,512]{2,1,0:T(8,128)(2,1)} %bitcast.17), calls=%async_computation.2 | async-start | bytes 2097152 | tf_op jit(solution)/shard_map/all_to_all | solution.py:490
  78.0 1.5 collective-permute-done.4.refs_1_.refs_6_
  79.5 16.3 %collective-permute-done.5.refs_2_.refs_7_ = bf16[256,640]{1,0:T(8,128)(2,1)} collective-permute-done((bf16[256,640]{1,0:T(8,128)(2,1)}, bf16[256,640]{1,0:T(8,128)(2,1)}, u32[]{:S(2)}, u32[]{:S(2)}) %collective-permute-start.5) | collective-permute-done | bytes 327712 | tf_op jit(solution)/shard_map/ppermute | solution.py:485
  95.8 2.0 %turn_step.1.refs_8_ = f32[1280,128]{1,0:T(8,128)} custom-call(bf16[40,1280]{1,0:T(8,128)(2,1)} %get-tuple-element.18.z, bf16[256,640]{1,0:T(8,128)(2,1)} %collective-permute-done.3.refs_0_.refs_5_, bf16[256,640]{1,0:T(8,128)(2,1)} %collective-permute-done.4.refs_1_.refs_6_, bf16[256,640]{1,0:T(8,128)(2,1)} %collective-permute-done.5.refs_2_.refs_7_), custom_call_target="tpu_custom_call" | custom-call | flops 12000000000 | bytes 7000000 | tf_op jit(solution)/shard_map/turn_step/pallas_call | solution.py:265
  97.9 0.8 copy-done.8
  99.2 8.6 %merge_step.1 = bf16[1024,1280]{1,0:T(8,128)(2,1)} custom-call(bf16[256,1280]{1,0:T(8,128)(2,1)} %bitcast.21, bf16[256,1280]{1,0:T(8,128)(2,1)} %copy-done.8, bf16[256,1280]{1,0:T(8,128)(2,1)} %copy-done.7, bf16[256,1280]{1,0:T(8,128)(2,1)} %copy-done.9, bf16[256,640]{1,0:T(8,128)(2,1)} %get-tuple-element.14.refs_4_, ...), custom_call_target="tpu_custom_call" | custom-call | flops 4000000000 | bytes 7000000 | tf_op jit(solution)/shard_map/merge_step/pallas_call | solution.py:332
  107.8 6.5 %all-to-all-start.3 = ((bf16[128,8,1280]{2,1,0:T(8,128)(2,1)}), bf16[128,8,1280]{2,1,0:T(8,128)(2,1)S(1)}, u32[]{:S(2)}, u32[]{:S(2)}) async-start(bf16[128,8,1280]{2,1,0:T(8,128)(2,1)} %bitcast.15), calls=%async_computation.3 | async-start | bytes 5242880 | tf_op jit(solution)/shard_map/all_to_all | solution.py:490
  114.4 2.5 %half_step.1.own = bf16[128,1280]{1,0:T(8,128)(2,1)} custom-call(bf16[1024,512]{1,0:T(8,128)(2,1)} %bitcast.14), custom_call_target="tpu_custom_call" | custom-call | flops 100000000 | bytes 1000000 | tf_op jit(solution)/shard_map/half_step/pallas_call | solution.py:367
  116.9 1.1 collective-permute-start.6
  117.9 1.5 collective-permute-done.6.other
  120.1 4.1 %vectors_step.1 = (bf16[256,1280]{1,0:T(8,128)(2,1)}, bf16[256,1280]{1,0:T(8,128)(2,1)}) custom-call(bf16[128,1280]{1,0:T(8,128)(2,1)} %half_step.1.own, bf16[128,1280]{1,0:T(8,128)(2,1)} %copy-done.10, bf16[1280,1280]{1,0:T(8,128)(2,1)} %wo.1), custom_call_target="tpu_custom_call" | custom-call | flops 2000000000 | bytes 6000000 | tf_op jit(solution)/shard_map/vectors_step/pallas_call | solution.py:391
  124.2 26.3 %all-to-all-done.3 = bf16[128,8,1280]{2,1,0:T(8,128)(2,1)S(1)} async-done(((bf16[128,8,1280]{2,1,0:T(8,128)(2,1)}), bf16[128,8,1280]{2,1,0:T(8,128)(2,1)S(1)}, u32[]{:S(2)}, u32[]{:S(2)}) %all-to-all-start.3) | async-done | bytes 2621472 | tf_op jit(solution)/shard_map/all_to_all | solution.py:490
  150.5 1.1 copy-done
  151.6 1.1 copy-done.1
  152.7 3.2 %final_step.1 = (f32[2,128,1280]{2,1,0:T(8,128)}, f32[10,4,1280]{2,1,0:T(4,128)}) custom-call(bf16[1024,1280]{1,0:T(8,128)(2,1)S(1)} %bitcast.12, bf16[256,1280]{1,0:T(8,128)(2,1)S(1)} %copy-done, bf16[256,1280]{1,0:T(8,128)(2,1)S(1)} %copy-done.1), custom_call_target="tpu_custom_call" | custom-call | flops 2000000000 | bytes 7000000 | tf_op jit(solution)/shard_map/final_step/pallas_call | solution.py:462
  (46 shorter events, 6.7 us)
Async XLA Ops:
  3.2 32.9 %copy-start.4 = (f32[1280]{0:T(1024)S(1)}, f32[1280]{0:T(1024)}, u32[]{:S(2)}) copy-start(f32[1280]{0:T(1024)} %param.17) | copy-start | bytes 15364
  3.2 34.1 %copy-start.5 = (s32[128,2]{0,1:T(2,128)S(1)}, s32[128,2]{0,1:T(2,128)}, u32[]{:S(2)}) copy-start(s32[128,2]{0,1:T(2,128)} %param.11) | copy-start | bytes 3076
  3.2 26.4 %all-to-all-start = ((bf16[128,2,1280]{2,1,0:T(2,128)(2,1)}), bf16[128,2,1280]{2,1,0:T(2,128)(2,1)S(1)}, u32[]{:S(2)}, u32[]{:S(2)}) async-start(bf16[128,2,1280]{2,1,0:T(2,128)(2,1)} %bitcast.11), calls=%async_computation | async-start | bytes 1310720 | tf_op jit(solution)/shard_map/all_to_all | solution.py:501
  15.7 35.4 %copy-start.6 = (s32[256]{0:T(256)}, s32[256]{0:T(256)S(1)}, u32[]{:S(2)}) copy-start(s32[256]{0:T(256)S(1)} %eq.41.pairs) | copy-start | bytes 3076
  31.4 19.7 %all-to-all-start.1 = ((bf16[128,2,1280]{2,1,0:T(2,128)(2,1)}), bf16[128,2,1280]{2,1,0:T(2,128)(2,1)S(1)}, u32[]{:S(2)}, u32[]{:S(2)}) async-start(bf16[128,2,1280]{2,1,0:T(2,128)(2,1)} %reshape.63), calls=%async_computation.1 | async-start | bytes 1310720 | tf_op jit(solution)/shard_map/all_to_all | solution.py:490
  51.1 0.8 copy-start.3
  51.1 22.0 %collective-permute-start.1 = (bf16[256,1280]{1,0:T(8,128)(2,1)S(1)}, bf16[256,1280]{1,0:T(8,128)(2,1)S(1)}, u32[]{:S(2)}, u32[]{:S(2)}) collective-permute-start(bf16[256,1280]{1,0:T(8,128)(2,1)S(1)} %bitcast.18), channel_id=1, source_target_pairs={{0,2},{1,3},{2,0},{3,1},{4,6},{5,7},{6,4},{7,5},{8,10},{9,11},{10,... | collective-permute-start | bytes 1966088 | tf_op jit(solution)/shard_map/ppermute | solution.py:485
  68.7 9.3 %collective-permute-start.3 = (bf16[256,640]{1,0:T(8,128)(2,1)}, bf16[256,640]{1,0:T(8,128)(2,1)}, u32[]{:S(2)}, u32[]{:S(2)}) collective-permute-start(bf16[256,640]{1,0:T(8,128)(2,1)} %get-tuple-element.15), channel_id=1, source_target_pairs={{0,1},{1,0},{2,3},{3,2},{4,5},{5,4},{6,7},{7,6},{8,9},{9,8},{10,11... | collective-permute-start | bytes 983048 | tf_op jit(solution)/shard_map/ppermute | solution.py:485
  69.9 9.6 %collective-permute-start.4 = (bf16[256,640]{1,0:T(8,128)(2,1)}, bf16[256,640]{1,0:T(8,128)(2,1)}, u32[]{:S(2)}, u32[]{:S(2)}) collective-permute-start(bf16[256,640]{1,0:T(8,128)(2,1)} %get-tuple-element.16), channel_id=1, source_target_pairs={{0,2},{1,3},{2,0},{3,1},{4,6},{5,7},{6,4},{7,5},{8,10},{9,11},{10,... | collective-permute-start | bytes 983048 | tf_op jit(solution)/shard_map/ppermute | solution.py:485
  71.1 24.7 %collective-permute-start.5 = (bf16[256,640]{1,0:T(8,128)(2,1)}, bf16[256,640]{1,0:T(8,128)(2,1)}, u32[]{:S(2)}, u32[]{:S(2)}) collective-permute-start(bf16[256,640]{1,0:T(8,128)(2,1)} %get-tuple-element.17), channel_id=1, source_target_pairs={{0,3},{1,2},{2,1},{3,0},{4,7},{5,6},{6,5},{7,4},{8,11},{9,10},{10,... | collective-permute-start | bytes 983048 | tf_op jit(solution)/shard_map/ppermute | solution.py:485
  72.9 24.9 %collective-permute-start = (bf16[256,1280]{1,0:T(8,128)(2,1)}, bf16[256,1280]{1,0:T(8,128)(2,1)S(1)}, u32[]{:S(2)}, u32[]{:S(2)}) collective-permute-start(bf16[256,1280]{1,0:T(8,128)(2,1)} %bitcast.20), channel_id=1, source_target_pairs={{0,1},{1,0},{2,3},{3,2},{4,5},{5,4},{6,7},{7,6},{8,9},{9,8},{10,11... | collective-permute-start | bytes 1966088 | tf_op jit(solution)/shard_map/ppermute | solution.py:485
  73.1 24.7 %copy-start.7 = (bf16[256,1280]{1,0:T(8,128)(2,1)}, bf16[256,1280]{1,0:T(8,128)(2,1)S(1)}, u32[]{:S(2)}) copy-start(bf16[256,1280]{1,0:T(8,128)(2,1)S(1)} %collective-permute-done.1.refs_2_) | copy-start | bytes 1966084
  73.1 24.7 %collective-permute-start.2 = (bf16[256,1280]{1,0:T(8,128)(2,1)S(1)}, bf16[256,1280]{1,0:T(8,128)(2,1)S(1)}, u32[]{:S(2)}, u32[]{:S(2)}) collective-permute-start(bf16[256,1280]{1,0:T(8,128)(2,1)S(1)} %collective-permute-done.1.refs_2_), channel_id=1, source_target_pairs={{0,1},{1,0},{2,3},{3,2},{4,5},{5,4},{6,7},{7,6},{8,9},{9,8},{10,11... | collective-permute-start | bytes 1966088 | tf_op jit(solution)/shard_map/ppermute | solution.py:485
  73.5 24.4 %all-to-all-start.2 = ((bf16[128,8,512]{2,1,0:T(8,128)(2,1)}), bf16[128,8,512]{2,1,0:T(8,128)(2,1)S(1)}, u32[]{:S(2)}, u32[]{:S(2)}) async-start(bf16[128,8,512]{2,1,0:T(8,128)(2,1)} %bitcast.17), calls=%async_computation.2 | async-start | bytes 2097152 | tf_op jit(solution)/shard_map/all_to_all | solution.py:490
  97.8 0.8 copy-start.8
  97.8 1.1 copy-start.9
  97.9 1.4 copy-start.2
  107.8 42.6 %all-to-all-start.3 = ((bf16[128,8,1280]{2,1,0:T(8,128)(2,1)}), bf16[128,8,1280]{2,1,0:T(8,128)(2,1)S(1)}, u32[]{:S(2)}, u32[]{:S(2)}) async-start(bf16[128,8,1280]{2,1,0:T(8,128)(2,1)} %bitcast.15), calls=%async_computation.3 | async-start | bytes 5242880 | tf_op jit(solution)/shard_map/all_to_all | solution.py:490
  116.9 2.5 %collective-permute-start.6 = (bf16[128,1280]{1,0:T(8,128)(2,1)}, bf16[128,1280]{1,0:T(8,128)(2,1)S(1)}, u32[]{:S(2)}, u32[]{:S(2)}) collective-permute-start(bf16[128,1280]{1,0:T(8,128)(2,1)} %half_step.1.own), channel_id=1, source_target_pairs={{0,1},{1,0},{2,3},{3,2},{4,5},{5,4},{6,7},{7,6},{8,9},{9,8},{10,11... | collective-permute-start | bytes 983048 | tf_op jit(solution)/shard_map/ppermute | solution.py:485
  119.4 0.7 copy-start.10
  150.5 1.1 copy-start
  151.6 1.1 copy-start.1
